TPU v7x, 32 devices: a whole 2x2x4 slice. The times are simulated.
32 devices in a mesh: dp: 8 (over z, y), ctx: 4 (over x, core).
Axes of the slice: x: 2, y: 2, z: 4, core: 2. Of those that a mesh axis runs over, the one named last changes fastest.
Arguments:
- tokens: bfloat16 [16, 1024, 1024], P('dp', 'ctx'), may hold values from -6 to 6
- segments: int32 [16, 1024], P('dp', 'ctx'), may hold values from 0 to 2, as said below
- pre_gain: bfloat16 [1024], P(('dp', 'ctx')), may hold values from 0.5 to 1.5
- gate_proj: bfloat16 [1024, 1536], P(('dp', 'ctx')), may hold values from -0.1875 to 0.1875
- mix_proj: bfloat16 [1024, 1792], P(('dp', 'ctx')), may hold values from -0.1875 to 0.1875
- step_proj: bfloat16 [1024, 24], P(('dp', 'ctx')), may hold values from -0.1875 to 0.1875
- conv_taps: bfloat16 [4, 1792], P(None, ('dp', 'ctx')), may hold values from -3 to 3
- conv_bias: bfloat16 [1792], P(('dp', 'ctx')), may hold values from -2 to 2
- decay_log: float32 [24], replicated, may hold values from -7.5 to -2.5
- step_bias: float32 [24], replicated, may hold values from -3 to -0.5
- skip_scale: float32 [24], replicated, may hold values from 0.5 to 1.5
- inner_gain: bfloat16 [1536], P(('dp', 'ctx')), may hold values from 0.5 to 1.5
- mamba_proj: bfloat16 [1536, 1024], P(('dp', 'ctx')), may hold values from -0.15625 to 0.15625
- query_proj: bfloat16 [1024, 1024], P(('dp', 'ctx')), may hold values from -0.1875 to 0.1875
- key_proj: bfloat16 [1024, 256], P(('dp', 'ctx')), may hold values from -0.1875 to 0.1875
- value_proj: bfloat16 [1024, 256], P(('dp', 'ctx')), may hold values from -0.1875 to 0.1875
- attn_proj: bfloat16 [1024, 1024], P(('dp', 'ctx')), may hold values from -0.75 to 0.75
- feed_gain: bfloat16 [1024], P(('dp', 'ctx')), may hold values from 0.5 to 1.5
- feed_gate: bfloat16 [1024, 2048], P(('dp', 'ctx')), may hold values from -0.1875 to 0.1875
- feed_up: bfloat16 [1024, 2048], P(('dp', 'ctx')), may hold values from -0.1875 to 0.1875
- feed_down: bfloat16 [2048, 1024], P(('dp', 'ctx')), may hold values from -0.125 to 0.125
- cotangent: bfloat16 [16, 1024, 1024], P('dp', 'ctx'), may hold values from -6 to 6
Outputs:
- output: bfloat16 [16, 1024, 1024], P('dp', 'ctx')
- grad_tokens: float32 [16, 1024, 1024], P('dp', 'ctx')
- grad_pre_gain: float32 [1024], P(('dp', 'ctx'))
- grad_gate_proj: float32 [1024, 1536], P(('dp', 'ctx'))
- grad_mix_proj: float32 [1024, 1792], P(('dp', 'ctx'))
- grad_step_proj: float32 [1024, 24], P(('dp', 'ctx'))
- grad_conv_taps: float32 [4, 1792], P(None, ('dp', 'ctx'))
- grad_conv_bias: float32 [1792], P(('dp', 'ctx'))
- grad_decay_log: float32 [24], replicated
- grad_step_bias: float32 [24], replicated
- grad_skip_scale: float32 [24], replicated
- grad_inner_gain: float32 [1536], P(('dp', 'ctx'))
- grad_mamba_proj: float32 [1536, 1024], P(('dp', 'ctx'))
- grad_query_proj: float32 [1024, 1024], P(('dp', 'ctx'))
- grad_key_proj: float32 [1024, 256], P(('dp', 'ctx'))
- grad_value_proj: float32 [1024, 256], P(('dp', 'ctx'))
- grad_attn_proj: float32 [1024, 1024], P(('dp', 'ctx'))
- grad_feed_gain: float32 [1024], P(('dp', 'ctx'))
- grad_feed_gate: float32 [1024, 2048], P(('dp', 'ctx'))
- grad_feed_up: float32 [1024, 2048], P(('dp', 'ctx'))
- grad_feed_down: float32 [2048, 1024], P(('dp', 'ctx'))
Inputs may be any that keep to these rules, and one draw needn't show every extreme that they name: `segments`: each sequence's segment numbers start at 0 and rise by one at each new document; every document has at least 1024 // 3 - 2 * (64) tokens. In each group of 2 sequences on one index of dp, one sequence is a single document and another holds three.
All inputs are finite; a program needn't handle non-finite values.
Results may differ from a plain program's by a relative error of at most 0.015.
Values may be sent and summed in bfloat16 or wider, within the bound.
A program may use at most 256 MiB of HBM per device.

v0:
```python
import jax
import jax.numpy as jnp
from jax import lax
from jax.sharding import PartitionSpec as P

MH = 24
MP = 64
DS = 128
KC = 4
QH = 8
KVH = 2
HD = 128


epsilon = 1e-05
highest = lax.Precision.HIGHEST
rope_base = 100000000000.0
masked_score = -1e30


def shifted(block, axis, distance):
    devices = range(lax.axis_size(axis))
    route = [(i - distance, i) for i in devices if i - distance in devices]
    return lax.ppermute(block, axis, route)


def prefix(value, axis, combine, identity):
    size, here = (lax.axis_size(axis), lax.axis_index(axis))
    everything = jax.tree.map(
        lambda part, kind: lax.all_gather(part.astype(kind), axis),
        value,
        (jnp.bfloat16, jnp.bfloat16),
    )
    start = jax.tree.map(
        lambda part, zero: jnp.broadcast_to(jnp.asarray(zero, part.dtype), part.shape),
        value,
        identity,
    )

    def prefix_hop(k, before):
        reached = k < here
        new = combine(
            before, jax.tree.map(lambda part, own: part[k].astype(own.dtype), everything, value)
        )
        return jax.tree.map(lambda a, b: jnp.where(reached, a, b), new, before)

    return lax.fori_loop(0, size, prefix_hop, start)


def entering(value, axis, combine, identity):
    size, here = (lax.axis_size(axis), lax.axis_index(axis))
    everything = jax.tree.map(
        lambda part, kind: lax.all_gather(part.astype(kind), axis),
        value,
        jax.tree.map(lambda a: jnp.bfloat16 if a.dtype == jnp.float32 else a.dtype, value),
    )
    start = jax.tree.map(
        lambda part, zero: jnp.broadcast_to(jnp.asarray(zero, part.dtype), part.shape),
        value,
        identity,
    )

    def entering_hop(k, before):
        at = size - 1 - k
        reached = at > here
        new = combine(
            before, jax.tree.map(lambda part, own: part[at].astype(own.dtype), everything, value)
        )
        return jax.tree.map(lambda a, b: jnp.where(reached, a, b), new, before)

    return lax.fori_loop(0, size, entering_hop, start)


def rms_scale(features):
    return lax.rsqrt(jnp.mean(features * features, axis=-1, keepdims=True) + epsilon)


def gained_norm(features, gain_vec):
    return features * rms_scale(features) * gain_vec


def forward_mul(left, right):
    return jnp.dot(left, right, preferred_element_type=jnp.float32)


def outer_sum(left, right):
    return lax.dot_general(
        left, right, (((0,), (0,)), ((), ())), preferred_element_type=jnp.float32
    )


def back_mul(grad_rows, weight):
    return lax.dot_general(
        grad_rows, weight, (((1,), (1,)), ((), ())), preferred_element_type=jnp.float32
    )


def rotate(features, positions, direction):
    head_size = features.shape[-1]
    half_size = head_size // 2
    freq_exp = lax.broadcasted_iota(jnp.int32, (half_size,), 0).astype(positions.dtype) * (
        2.0 / head_size
    )
    inverse = jnp.power(rope_base, -freq_exp)
    angles = positions[:, None] * inverse[None, :]
    cosine = jnp.cos(angles)[:, None, :]
    sine_part = direction * jnp.sin(angles)[:, None, :]
    first_half = features[..., :half_size]
    second_half = features[..., half_size:]
    return jnp.concatenate(
        [
            first_half * cosine - second_half * sine_part,
            second_half * cosine + first_half * sine_part,
        ],
        axis=-1,
    )


def conv_local(extended, segment_wide, conv_taps, conv_bias):
    tap_count = conv_taps.shape[0]
    length_now = extended.shape[1] - tap_count + 1
    segment_now = segment_wide[:, tap_count - 1 :]
    conv_total = conv_bias
    for offset in range(tap_count):
        window = extended[:, offset : offset + length_now]
        same_doc = (segment_wide[:, offset : offset + length_now] == segment_now)[..., None]
        conv_total = conv_total + conv_taps[offset] * jnp.where(same_doc, window, 0.0)
    return conv_total


def prepare(extended, segment_wide, step_raw, conv_taps, conv_bias, step_bias, decay_log):
    activated = jax.nn.silu(conv_local(extended, segment_wide, conv_taps, conv_bias))
    inner_width = MH * MP
    inner_vals = activated[..., :inner_width].reshape(activated.shape[:-1] + (MH, MP))
    input_map = activated[..., inner_width : inner_width + DS]
    output_map = activated[..., inner_width + DS :]
    step_size = jax.nn.softplus(step_raw + step_bias)
    log_decay = -jnp.exp(decay_log) * step_size
    return (inner_vals, input_map, output_map, step_size, log_decay)


def block_output(
    step_size, log_decay, inner_vals, input_map, output_map, segment_ids, start_flag, state_in
):
    count_rows = log_decay.shape[0]
    cumulative = jnp.cumsum(log_decay, axis=0)
    carried = (jnp.cumsum(start_flag) == 0).astype(cumulative.dtype)
    row_index = lax.broadcasted_iota(jnp.int32, (count_rows, count_rows), 0)
    col_index = lax.broadcasted_iota(jnp.int32, (count_rows, count_rows), 1)
    allowed = ((col_index <= row_index) & (segment_ids[:, None] == segment_ids[None, :]))[
        :, :, None
    ]
    spread = cumulative[:, None, :] - cumulative[None, :, :]
    mixing = jnp.where(allowed, jnp.exp(jnp.where(allowed, spread, 0.0)), 0.0)
    affinity = jnp.dot(output_map, input_map.T, precision=highest)
    kernel = affinity[:, :, None] * mixing * step_size[None, :, :]
    result = jnp.einsum("ijh,jhp->ihp", kernel, inner_vals, precision=highest)
    entry_scale = carried[:, None] * jnp.exp(cumulative)
    carried_in = jnp.einsum("is,hps->ihp", output_map, state_in, precision=highest)
    return result + entry_scale[:, :, None] * carried_in


def block_summary(step_size, log_decay, inner_vals, input_map, segment_ids, start_flag):
    cumulative = jnp.cumsum(log_decay, axis=0)
    last_cum = cumulative[-1]
    keep_last = (jnp.sum(start_flag) == 0).astype(cumulative.dtype)
    block_decay = keep_last * jnp.exp(last_cum)
    same_last = (segment_ids == segment_ids[-1])[:, None]
    final_weight = jnp.where(same_last, jnp.exp(last_cum[None, :] - cumulative), 0.0) * step_size
    local_state = jnp.einsum(
        "jh,jhp,js->hps", final_weight, inner_vals, input_map, precision=highest
    )
    return (block_decay, local_state)


def mamba_tail(result, inner_vals, gate_mamba, skip_scale, inner_gain):
    full_out = result + skip_scale[:, None] * inner_vals
    gated_out = full_out.reshape(full_out.shape[:-2] + (MH * MP,)) * jax.nn.silu(gate_mamba)
    return gained_norm(gated_out, inner_gain)


def chain_combine(earlier, later):
    return (earlier[0] * later[0], later[0][..., None, None] * earlier[1] + later[1])


def attention_mask(positions, segment_ids, segment_all):
    key_count = segment_all.shape[1]
    key_pos = lax.broadcasted_iota(jnp.int32, (key_count,), 0).astype(jnp.float32)
    causal = key_pos[None, :] <= positions[:, None]
    same_doc = segment_ids[:, :, None] == segment_all[:, None, :]
    return (causal[None] & same_doc)[:, None, None]


def score_block(grouped, keys_all, allowed):
    scores = jnp.einsum(
        "sikgd,sjkd->skgij", grouped, keys_all, preferred_element_type=jnp.float32
    ) * HD ** (-0.5)
    return jnp.where(allowed, scores, masked_score)


def body(
    tokens,
    segments,
    pre_gain,
    gate_proj,
    mix_proj,
    step_proj,
    conv_taps,
    conv_bias,
    decay_log,
    step_bias,
    skip_scale,
    inner_gain,
    mamba_proj,
    query_proj,
    key_proj,
    value_proj,
    attn_proj,
    feed_gain,
    feed_gate,
    feed_up,
    feed_down,
    cotangent,
):
    gathered = (
        lax.all_gather(pre_gain, ("dp", "ctx"), axis=0, tiled=True),
        lax.all_gather(gate_proj, ("dp", "ctx"), axis=0, tiled=True),
        lax.all_gather(mix_proj, ("dp", "ctx"), axis=0, tiled=True),
        lax.all_gather(step_proj, ("dp", "ctx"), axis=0, tiled=True),
        lax.all_gather(conv_taps, ("dp", "ctx"), axis=1, tiled=True),
        lax.all_gather(conv_bias, ("dp", "ctx"), axis=0, tiled=True),
        lax.all_gather(inner_gain, ("dp", "ctx"), axis=0, tiled=True),
        lax.all_gather(mamba_proj, ("dp", "ctx"), axis=0, tiled=True),
        lax.all_gather(query_proj, ("dp", "ctx"), axis=0, tiled=True),
        lax.all_gather(key_proj, ("dp", "ctx"), axis=0, tiled=True),
        lax.all_gather(value_proj, ("dp", "ctx"), axis=0, tiled=True),
        lax.all_gather(attn_proj, ("dp", "ctx"), axis=0, tiled=True),
        lax.all_gather(feed_gain, ("dp", "ctx"), axis=0, tiled=True),
        lax.all_gather(feed_gate, ("dp", "ctx"), axis=0, tiled=True),
        lax.all_gather(feed_up, ("dp", "ctx"), axis=0, tiled=True),
        lax.all_gather(feed_down, ("dp", "ctx"), axis=0, tiled=True),
    )
    seq_count, block_rows, model_width = tokens.shape
    tap_count = KC
    inner_width = MH * MP
    group_size = QH // KVH
    ctx_index = lax.axis_index("ctx")
    flat_rows = tokens.reshape(seq_count * block_rows, model_width).astype(jnp.float32)
    normed = gained_norm(flat_rows, gathered[0].astype(jnp.float32)).astype(jnp.bfloat16)
    gate_mamba = forward_mul(normed, gathered[1]).reshape(seq_count, block_rows, inner_width)
    conv_input = forward_mul(normed, gathered[2]).reshape(seq_count, block_rows, -1)
    step_raw = forward_mul(normed, gathered[3]).reshape(seq_count, block_rows, MH)
    segment_ids = segments.astype(jnp.float32)
    prev_rows, prev_segment = shifted(
        (conv_input[:, block_rows - tap_count + 1 :], segment_ids[:, block_rows - tap_count + 1 :]),
        "ctx",
        1,
    )
    extended = jnp.concatenate([prev_rows, conv_input], axis=1)
    segment_wide = jnp.concatenate([prev_segment, segment_ids], axis=1)
    start_flag = (
        segment_ids != segment_wide[:, tap_count - 2 : tap_count - 2 + block_rows]
    ).astype(jnp.float32)
    taps_float = gathered[4].astype(jnp.float32)
    conv_bias_float = gathered[5].astype(jnp.float32)
    inner_gain_float = gathered[6].astype(jnp.float32)
    inner_vals, input_map, output_map, step_size, log_decay = prepare(
        extended, segment_wide, step_raw, taps_float, conv_bias_float, step_bias, decay_log
    )
    block_decay, local_state = jax.vmap(block_summary)(
        step_size, log_decay, inner_vals, input_map, segment_ids, start_flag
    )
    identity_pair = (jnp.ones_like(block_decay), jnp.zeros_like(local_state))
    carried = prefix((block_decay, local_state), "ctx", chain_combine, identity_pair)
    state_in = carried[1]
    result = jax.vmap(block_output)(
        step_size, log_decay, inner_vals, input_map, output_map, segment_ids, start_flag, state_in
    )
    mixed_low = mamba_tail(result, inner_vals, gate_mamba, skip_scale, inner_gain_float).astype(
        jnp.bfloat16
    )
    branch_mamba = forward_mul(mixed_low.reshape(-1, inner_width), gathered[7])
    positions = (ctx_index * block_rows + lax.broadcasted_iota(jnp.int32, (block_rows,), 0)).astype(
        jnp.float32
    )
    query_pre = forward_mul(normed, gathered[8]).reshape(seq_count, block_rows, QH, HD)
    key_pre = forward_mul(normed, gathered[9]).reshape(seq_count, block_rows, KVH, HD)
    value_pre = forward_mul(normed, gathered[10]).reshape(seq_count, block_rows, KVH, HD)
    queries = rotate(query_pre, positions, 1.0).astype(jnp.bfloat16)
    keys_rot = rotate(key_pre, positions, 1.0).astype(jnp.bfloat16)
    values = value_pre.astype(jnp.bfloat16)
    keys_all, values_all, segment_all = (
        lax.all_gather(keys_rot, "ctx", axis=1, tiled=True),
        lax.all_gather(values, "ctx", axis=1, tiled=True),
        lax.all_gather(segment_ids.astype(jnp.bfloat16), "ctx", axis=1, tiled=True),
    )
    grouped = queries.reshape(seq_count, block_rows, KVH, group_size, HD)
    allowed = attention_mask(positions, segment_ids, segment_all.astype(jnp.float32))
    scores = score_block(grouped, keys_all, allowed)
    row_max = jnp.max(scores, axis=-1, keepdims=True)
    log_total = row_max + jnp.log(jnp.sum(jnp.exp(scores - row_max), axis=-1, keepdims=True))
    attend = jnp.exp(scores - log_total).astype(jnp.bfloat16)
    attended = jnp.einsum(
        "skgij,sjkd->sikgd", attend, values_all, preferred_element_type=jnp.float32
    ).astype(jnp.bfloat16)
    branch_attn = forward_mul(attended.reshape(-1, QH * HD), gathered[11])
    residual = flat_rows + branch_mamba + branch_attn
    feed_scale = gathered[12].astype(jnp.float32)
    normed_two = gained_norm(residual, feed_scale).astype(jnp.bfloat16)
    feed_gate_out = forward_mul(normed_two, gathered[13])
    feed_up_out = forward_mul(normed_two, gathered[14])
    feed_hidden = (jax.nn.silu(feed_gate_out) * feed_up_out).astype(jnp.bfloat16)
    output = (
        (residual + forward_mul(feed_hidden, gathered[15]))
        .astype(jnp.bfloat16)
        .reshape(seq_count, block_rows, model_width)
    )
    again_weights = (
        lax.all_gather(pre_gain, ("dp", "ctx"), axis=0, tiled=True),
        lax.all_gather(gate_proj, ("dp", "ctx"), axis=0, tiled=True),
        lax.all_gather(mix_proj, ("dp", "ctx"), axis=0, tiled=True),
        lax.all_gather(step_proj, ("dp", "ctx"), axis=0, tiled=True),
        lax.all_gather(conv_taps, ("dp", "ctx"), axis=1, tiled=True),
        lax.all_gather(conv_bias, ("dp", "ctx"), axis=0, tiled=True),
        lax.all_gather(inner_gain, ("dp", "ctx"), axis=0, tiled=True),
        lax.all_gather(mamba_proj, ("dp", "ctx"), axis=0, tiled=True),
        lax.all_gather(query_proj, ("dp", "ctx"), axis=0, tiled=True),
        lax.all_gather(key_proj, ("dp", "ctx"), axis=0, tiled=True),
        lax.all_gather(value_proj, ("dp", "ctx"), axis=0, tiled=True),
        lax.all_gather(attn_proj, ("dp", "ctx"), axis=0, tiled=True),
        lax.all_gather(feed_gain, ("dp", "ctx"), axis=0, tiled=True),
        lax.all_gather(feed_gate, ("dp", "ctx"), axis=0, tiled=True),
        lax.all_gather(feed_up, ("dp", "ctx"), axis=0, tiled=True),
        lax.all_gather(feed_down, ("dp", "ctx"), axis=0, tiled=True),
    )
    upstream = cotangent.reshape(-1, model_width)
    grad_feed_down = outer_sum(feed_hidden, upstream)
    grad_hidden = back_mul(upstream, again_weights[15])
    _, swiglu_back = jax.vjp(
        lambda gate_arg, up_arg: jax.nn.silu(gate_arg) * up_arg, feed_gate_out, feed_up_out
    )
    grad_gate_ff, grad_up_ff = swiglu_back(grad_hidden)
    gate_ff_low = grad_gate_ff.astype(jnp.bfloat16)
    up_ff_low = grad_up_ff.astype(jnp.bfloat16)
    grad_feed_gate = outer_sum(normed_two, gate_ff_low)
    grad_feed_up = outer_sum(normed_two, up_ff_low)
    grad_normed_two = back_mul(gate_ff_low, again_weights[13]) + back_mul(
        up_ff_low, again_weights[14]
    )
    _, norm_two_back = jax.vjp(gained_norm, residual, again_weights[12].astype(jnp.float32))
    grad_res_norm, grad_feed_gain = norm_two_back(grad_normed_two)
    grad_residual = upstream.astype(jnp.float32) + grad_res_norm
    residual_low = grad_residual.astype(jnp.bfloat16)
    grad_mamba_proj = outer_sum(mixed_low.reshape(-1, inner_width), residual_low)
    grad_attn_proj = outer_sum(attended.reshape(-1, QH * HD), residual_low)
    grad_mixed = back_mul(residual_low, again_weights[7]).reshape(
        seq_count, block_rows, inner_width
    )
    grad_attended = (
        back_mul(residual_low, again_weights[11])
        .astype(jnp.bfloat16)
        .reshape(seq_count, block_rows, KVH, group_size, HD)
    )
    scores_again = score_block(grouped, keys_all, allowed)
    attend_full = jnp.exp(scores_again - log_total)
    attend_again = attend_full.astype(jnp.bfloat16)
    grad_attend = jnp.einsum(
        "sikgd,sjkd->skgij", grad_attended, values_all, preferred_element_type=jnp.float32
    )
    grad_values_all = jnp.einsum(
        "skgij,sikgd->sjkd", attend_again, grad_attended, preferred_element_type=jnp.float32
    )
    row_dot = jnp.sum(attend_full * grad_attend, axis=-1, keepdims=True)
    grad_scores = (attend_full * (grad_attend - row_dot)).astype(jnp.bfloat16)
    grad_queries = jnp.einsum(
        "skgij,sjkd->sikgd", grad_scores, keys_all, preferred_element_type=jnp.float32
    ) * HD ** (-0.5)
    grad_keys_all = jnp.einsum(
        "skgij,sikgd->sjkd", grad_scores, grouped, preferred_element_type=jnp.float32
    ) * HD ** (-0.5)
    grad_keys, grad_values = (
        lax.psum_scatter(
            grad_keys_all.astype(jnp.bfloat16), "ctx", scatter_dimension=1, tiled=True
        ).astype(jnp.float32),
        lax.psum_scatter(
            grad_values_all.astype(jnp.bfloat16), "ctx", scatter_dimension=1, tiled=True
        ).astype(jnp.float32),
    )
    query_low = (
        rotate(grad_queries.reshape(seq_count, block_rows, QH, HD), positions, -1.0)
        .astype(jnp.bfloat16)
        .reshape(-1, QH * HD)
    )
    key_low = rotate(grad_keys, positions, -1.0).astype(jnp.bfloat16).reshape(-1, KVH * HD)
    value_low = grad_values.astype(jnp.bfloat16).reshape(-1, KVH * HD)
    grad_query_proj = outer_sum(normed, query_low)
    grad_key_proj = outer_sum(normed, key_low)
    grad_value_proj = outer_sum(normed, value_low)
    mamba_args = (
        extended,
        step_raw,
        again_weights[4].astype(jnp.float32),
        again_weights[5].astype(jnp.float32),
        step_bias,
        decay_log,
        state_in,
        gate_mamba,
        skip_scale,
        again_weights[6].astype(jnp.float32),
    )

    def mamba_front(
        extended_in,
        step_in,
        taps_in,
        conv_bias_in,
        step_bias_in,
        decay_log_in,
        state_arg,
        gate_in,
        skip_in,
        gain_in,
    ):
        prepared = prepare(
            extended_in, segment_wide, step_in, taps_in, conv_bias_in, step_bias_in, decay_log_in
        )
        result_in = jax.vmap(block_output)(
            prepared[3],
            prepared[4],
            prepared[0],
            prepared[1],
            prepared[2],
            segment_ids,
            start_flag,
            state_arg,
        )
        return mamba_tail(result_in, prepared[0], gate_in, skip_in, gain_in)

    def summary_front(extended_in, step_in, taps_in, conv_bias_in, step_bias_in, decay_log_in):
        prepared = prepare(
            extended_in, segment_wide, step_in, taps_in, conv_bias_in, step_bias_in, decay_log_in
        )
        return jax.vmap(block_summary)(
            prepared[3], prepared[4], prepared[0], prepared[1], segment_ids, start_flag
        )

    _, front_back = jax.vjp(mamba_front, *mamba_args)
    front_grads = front_back(grad_mixed)
    chain_grads = entering((block_decay, front_grads[6]), "ctx", chain_combine, identity_pair)
    grad_state_out = chain_grads[1]
    grad_decay = jnp.sum(grad_state_out * state_in, axis=(2, 3))
    _, summary_back = jax.vjp(summary_front, *mamba_args[:6])
    summary_grads = summary_back((grad_decay, grad_state_out))
    grad_extended = front_grads[0] + summary_grads[0]
    grad_step_raw = front_grads[1] + summary_grads[1]
    grad_conv_taps = front_grads[2] + summary_grads[2]
    grad_conv_bias = front_grads[3] + summary_grads[3]
    grad_step_bias = front_grads[4] + summary_grads[4]
    grad_decay_log = front_grads[5] + summary_grads[5]
    back_rows = shifted(grad_extended[:, : tap_count - 1].astype(jnp.bfloat16), "ctx", -1).astype(
        jnp.float32
    )
    grad_conv_input = (
        grad_extended[:, tap_count - 1 :].at[:, block_rows - tap_count + 1 :].add(back_rows)
    )
    gate_low = front_grads[7].astype(jnp.bfloat16).reshape(-1, inner_width)
    conv_low = grad_conv_input.astype(jnp.bfloat16).reshape(-1, grad_conv_input.shape[-1])
    step_low = grad_step_raw.astype(jnp.bfloat16).reshape(-1, MH)
    grad_gate_proj = outer_sum(normed, gate_low)
    grad_mix_proj = outer_sum(normed, conv_low)
    grad_step_proj = outer_sum(normed, step_low)
    grad_normed = (
        back_mul(gate_low, again_weights[1])
        + back_mul(conv_low, again_weights[2])
        + back_mul(step_low, again_weights[3])
    )
    grad_normed = (
        grad_normed
        + back_mul(query_low, again_weights[8])
        + back_mul(key_low, again_weights[9])
        + back_mul(value_low, again_weights[10])
    )
    _, norm_one_back = jax.vjp(gained_norm, flat_rows, again_weights[0].astype(jnp.float32))
    grad_flat, grad_pre_gain = norm_one_back(grad_normed)
    grad_tokens = (grad_residual + grad_flat).reshape(seq_count, block_rows, model_width)
    summed = (
        lax.psum_scatter(grad_pre_gain, ("dp", "ctx"), scatter_dimension=0, tiled=True),
        lax.psum_scatter(grad_gate_proj, ("dp", "ctx"), scatter_dimension=0, tiled=True),
        lax.psum_scatter(grad_mix_proj, ("dp", "ctx"), scatter_dimension=0, tiled=True),
        lax.psum_scatter(grad_step_proj, ("dp", "ctx"), scatter_dimension=0, tiled=True),
        lax.psum_scatter(grad_conv_taps, ("dp", "ctx"), scatter_dimension=1, tiled=True),
        lax.psum_scatter(grad_conv_bias, ("dp", "ctx"), scatter_dimension=0, tiled=True),
        lax.psum_scatter(front_grads[9], ("dp", "ctx"), scatter_dimension=0, tiled=True),
        lax.psum_scatter(grad_mamba_proj, ("dp", "ctx"), scatter_dimension=0, tiled=True),
        lax.psum_scatter(grad_query_proj, ("dp", "ctx"), scatter_dimension=0, tiled=True),
        lax.psum_scatter(grad_key_proj, ("dp", "ctx"), scatter_dimension=0, tiled=True),
        lax.psum_scatter(grad_value_proj, ("dp", "ctx"), scatter_dimension=0, tiled=True),
        lax.psum_scatter(grad_attn_proj, ("dp", "ctx"), scatter_dimension=0, tiled=True),
        lax.psum_scatter(grad_feed_gain, ("dp", "ctx"), scatter_dimension=0, tiled=True),
        lax.psum_scatter(grad_feed_gate, ("dp", "ctx"), scatter_dimension=0, tiled=True),
        lax.psum_scatter(grad_feed_up, ("dp", "ctx"), scatter_dimension=0, tiled=True),
        lax.psum_scatter(grad_feed_down, ("dp", "ctx"), scatter_dimension=0, tiled=True),
    )
    head_sums = lax.psum((grad_decay_log, grad_step_bias, front_grads[8]), ("dp", "ctx"))
    return (
        output,
        grad_tokens,
        summed[0],
        summed[1],
        summed[2],
        summed[3],
        summed[4],
        summed[5],
        head_sums[0],
        head_sums[1],
        head_sums[2],
        summed[6],
        summed[7],
        summed[8],
        summed[9],
        summed[10],
        summed[11],
        summed[12],
        summed[13],
        summed[14],
        summed[15],
    )


def solution(mesh):
    return jax.shard_map(
        body,
        mesh=mesh,
        in_specs=(
            P("dp", "ctx", None),
            P("dp", "ctx"),
            P(("dp", "ctx")),
            P(("dp", "ctx"), None),
            P(("dp", "ctx"), None),
            P(("dp", "ctx"), None),
            P(None, ("dp", "ctx")),
            P(("dp", "ctx")),
            P(),
            P(),
            P(),
            P(("dp", "ctx")),
            P(("dp", "ctx"), None),
            P(("dp", "ctx"), None),
            P(("dp", "ctx"), None),
            P(("dp", "ctx"), None),
            P(("dp", "ctx"), None),
            P(("dp", "ctx")),
            P(("dp", "ctx"), None),
            P(("dp", "ctx"), None),
            P(("dp", "ctx"), None),
            P("dp", "ctx", None),
        ),
        out_specs=(
            P("dp", "ctx", None),
            P("dp", "ctx", None),
            P(("dp", "ctx")),
            P(("dp", "ctx"), None),
            P(("dp", "ctx"), None),
            P(("dp", "ctx"), None),
            P(None, ("dp", "ctx")),
            P(("dp", "ctx")),
            P(),
            P(),
            P(),
            P(("dp", "ctx")),
            P(("dp", "ctx"), None),
            P(("dp", "ctx"), None),
            P(("dp", "ctx"), None),
            P(("dp", "ctx"), None),
            P(("dp", "ctx"), None),
            P(("dp", "ctx")),
            P(("dp", "ctx"), None),
            P(("dp", "ctx"), None),
            P(("dp", "ctx"), None),
        ),
        check_vma=False,
    )
```

profile of v0, /device:TPU:0, one launch (start us, length us, event | category | flops | bytes accessed | tf_op | source)
XLA Modules:
  0.0 2298.4 jit_solution(1689046800756136545)
XLA Ops:
  12.1 42.2 %all-reduce.32 = (bf16[1024]{0:T(1024)(128)(2,1)S(1)}, bf16[1792]{0:T(1024)(128)(2,1)S(1)}, bf16[1536]{0:T(1024)(128)(2,1)S(1)}, bf16[1024]{0:T(1024)(128)(2,1)}) all-reduce(bf16[1024]{0:T(1024)(128)(2,1)S(1)} %dynamic-update-slice.4, bf16[1792]{0:T(1024)(128)(2,1)S(1)} %dynamic-update-slice.3, ...), channel_id=1, replica_groups=mesh['dp'=8,'ctx'=4] {'dp','ctx'}, use_global_device_ids=true, to_apply=%add.23 | all-reduce | flops 5376 | bytes 21504
  54.3 42.8 %all_gather.105 = bf16[1024,256]{1,0:T(8,128)(2,1)S(1)} all-gather(bf16[32,256]{1,0:T(8,128)(2,1)} %param.43), channel_id=1, replica_groups=mesh['dp'=8,'ctx'=4] {'dp','ctx'}, dimensions={0}, use_global_device_ids=true | all-gather | bytes 540672 | tf_op jit(solution)/shard_map/all_gather | solution.py:235
  102.1 38.3 %all_gather.102 = bf16[1024,256]{1,0:T(8,128)(2,1)S(1)} all-gather(bf16[32,256]{1,0:T(8,128)(2,1)S(1)} %copy-done.96), channel_id=1, replica_groups=mesh['dp'=8,'ctx'=4] {'dp','ctx'}, dimensions={0}, use_global_device_ids=true | all-gather | bytes 540672 | tf_op jit(solution)/shard_map/all_gather | solution.py:236
  144.3 38.9 %all-gather.3 = bf16[32,32,24]{1,2,0:T(8,128)(2,1)S(1)} all-gather(bf16[1,32,24]{1,2,0:T(8,128)(2,1)S(1)} %bitcast.484), channel_id=1, replica_groups=mesh['dp'=8,'ctx'=4] {'dp','ctx'}, dimensions={0}, use_global_device_ids=true | all-gather | bytes 50688 | tf_op jit(solution)/shard_map/all_gather | solution.py:229
  189.8 36.7 %all-gather.2 = bf16[32,56,4]{1,2,0:T(4,128)(2,1)S(1)} all-gather(bf16[1,56,4]{1,2,0:T(4,128)(2,1)S(1)} %bitcast.486), channel_id=1, replica_groups=mesh['dp'=8,'ctx'=4] {'dp','ctx'}, dimensions={0}, use_global_device_ids=true | all-gather | bytes 14784 | tf_op jit(solution)/shard_map/all_gather | solution.py:230
  240.3 12.2 fusion.53
  273.2 7.1 all_gather.104
  305.4 11.3 fusion.21
  316.7 9.3 exponential_reduce_fusion
  326.0 11.4 fusion.96
  349.3 8.8 while.31
  361.9 15.9 fusion.57
  381.4 18.1 fusion.60
  403.0 7.9 multiply_reduce_fusion.15
  421.4 57.2 %all-gather.31.cloned.1.call-done = bf16[1024,2048]{1,0:T(8,128)(2,1)} async-done(((bf16[32,2048]{1,0:T(8,128)(2,1)}), bf16[1024,2048]{1,0:T(8,128)(2,1)}) %all-gather.31.cloned.1.call-update) | async-done | bytes 4194320 | tf_op jit(solution)/shard_map/all_gather | solution.py:239
  478.6 6.5 fusion.197
  485.1 56.8 %all-gather.33.cloned.1.call-done = bf16[1024,2048]{1,0:T(8,128)(2,1)} async-done(((bf16[32,2048]{1,0:T(8,128)(2,1)}), bf16[1024,2048]{1,0:T(8,128)(2,1)}) %all-gather.33.cloned.1.call-update) | async-done | bytes 4194320 | tf_op jit(solution)/shard_map/all_gather | solution.py:240
  541.9 6.8 fusion.198
  548.7 56.7 %all-gather.35.cloned.1.call-done = bf16[2048,1024]{1,0:T(8,128)(2,1)} async-done(((bf16[64,1024]{1,0:T(8,128)(2,1)}), bf16[2048,1024]{1,0:T(8,128)(2,1)}) %all-gather.35.cloned.1.call-update) | async-done | bytes 4194320 | tf_op jit(solution)/shard_map/all_gather | solution.py:241
  605.4 9.1 multiply_convert_fusion
  630.1 11.9 fusion.2
  642.1 12.8 fusion.4
  688.1 22.7 fusion.23
  722.8 11.6 fusion.98
  738.2 8.9 while.32
  747.1 6.5 broadcast_multiply_fusion
  760.0 6.3 reduce-window.46
  791.0 6.2 fusion.204
  822.2 7.5 fusion.206
  829.8 7.5 fusion.207
  837.6 7.5 fusion.208
  846.0 14.2 bitcast_add_fusion
  866.7 7.0 fusion.99
  879.3 7.1 fusion.102
  886.6 12.3 multiply_reduce_fusion.4
  898.9 8.0 multiply_select_fusion.4
  906.9 6.8 add_add_fusion.1
  948.3 42.4 %all-reduce.31 = (f32[1024]{0:T(1024)S(1)}, f32[4,1792]{1,0:T(4,128)S(1)}, f32[1792]{0:T(1024)S(1)}, f32[24]{0:T(128)}, f32[24]{0:T(128)}, /*index=5*/f32[24]{0:T(128)}, f32[1536]{0:T(1024)S(1)}, f32[1024]{0:T(1024)S(1)}) all-reduce(f32[1024]{0:T(1024)S(1)} %get-tuple-element.321, ...), channel_id=6, replica_groups=mesh['dp'=8,'ctx'=4] {'dp','ctx'}, use_global_device_ids=true, to_apply=%region_35.37.clone | all-reduce | flops 12616 | bytes 100928
  1000.0 49.7 %reduce-scatter.29.cloned.1.call-done = f32[32,256]{1,0:T(8,128)} async-done(((f32[1024,256]{1,0:T(8,128)}), f32[32,256]{1,0:T(8,128)}) %reduce-scatter.29.cloned.1.call-update) | async-done | bytes 32784 | tf_op jit(solution)/shard_map/reduce_scatter | solution.py:496
  1049.7 133.4 %reduce-scatter.31.cloned.1.call-done = f32[32,256]{1,0:T(8,128)} async-done(((f32[1024,256]{1,0:T(8,128)}), f32[32,256]{1,0:T(8,128)}) %reduce-scatter.31.cloned.1.call-update) | async-done | bytes 32784 | tf_op jit(solution)/shard_map/reduce_scatter | solution.py:497
  1183.1 117.6 %reduce-scatter.25.cloned.1.call-done = f32[48,1024]{1,0:T(8,128)} async-done(((f32[1536,1024]{1,0:T(8,128)}), f32[48,1024]{1,0:T(8,128)}) %reduce-scatter.25.cloned.1.call-update) | async-done | bytes 196624 | tf_op jit(solution)/shard_map/reduce_scatter | solution.py:494
  1300.7 120.0 %reduce-scatter.21.cloned.1.call-done = f32[32,1536]{1,0:T(8,128)} async-done(((f32[1024,1536]{1,0:T(8,128)}), f32[32,1536]{1,0:T(8,128)}) %reduce-scatter.21.cloned.1.call-update) | async-done | bytes 196624 | tf_op jit(solution)/shard_map/reduce_scatter | solution.py:488
  1420.8 143.0 %reduce-scatter.27.cloned.1.call-done = f32[32,1024]{1,0:T(8,128)} async-done(((f32[1024,1024]{1,0:T(8,128)}), f32[32,1024]{1,0:T(8,128)}) %reduce-scatter.27.cloned.1.call-update) | async-done | bytes 131088 | tf_op jit(solution)/shard_map/reduce_scatter | solution.py:495
  1563.7 139.8 %reduce-scatter.33.cloned.1.call-done = f32[32,1024]{1,0:T(8,128)} async-done(((f32[1024,1024]{1,0:T(8,128)}), f32[32,1024]{1,0:T(8,128)}) %reduce-scatter.33.cloned.1.call-update) | async-done | bytes 131088 | tf_op jit(solution)/shard_map/reduce_scatter | solution.py:498
  1703.6 147.5 %reduce-scatter.35.cloned.1.call-done = f32[32,2048]{1,0:T(8,128)} async-done(((f32[1024,2048]{1,0:T(8,128)}), f32[32,2048]{1,0:T(8,128)}) %reduce-scatter.35.cloned.1.call-update) | async-done | bytes 262160 | tf_op jit(solution)/shard_map/reduce_scatter | solution.py:500
  1851.0 147.6 %reduce-scatter.37.cloned.1.call-done = f32[32,2048]{1,0:T(8,128)} async-done(((f32[1024,2048]{1,0:T(8,128)}), f32[32,2048]{1,0:T(8,128)}) %reduce-scatter.37.cloned.1.call-update) | async-done | bytes 262160 | tf_op jit(solution)/shard_map/reduce_scatter | solution.py:501
  1998.7 147.4 %reduce-scatter.39.cloned.1.call-done = f32[64,1024]{1,0:T(8,128)} async-done(((f32[2048,1024]{1,0:T(8,128)}), f32[64,1024]{1,0:T(8,128)}) %reduce-scatter.39.cloned.1.call-update) | async-done | bytes 262160 | tf_op jit(solution)/shard_map/reduce_scatter | solution.py:502
  2146.1 145.5 %reduce-scatter.23.cloned.1.call-done = f32[32,1792]{1,0:T(8,128)} async-done(((f32[1024,1792]{1,0:T(8,128)}), f32[32,1792]{1,0:T(8,128)}) %reduce-scatter.23.cloned.1.call-update) | async-done | bytes 229392 | tf_op jit(solution)/shard_map/reduce_scatter | solution.py:489
  (545 shorter events, 306.9 us)
Async XLA Ops:
  7.2 93.2 %copy-start.13 = (bf16[2,256,1024]{2,1,0:T(8,128)(2,1)S(1)}, bf16[2,256,1024]{2,1,0:T(8,128)(2,1)}, u32[]{:S(2)}) copy-start(bf16[2,256,1024]{2,1,0:T(8,128)(2,1)} %param.29) | copy-start | bytes 3145732
  7.2 223.7 %all-gather.17.cloned.1.call-start = ((), (), s32[]{:S(2)}) async-start(), calls=%async_computation.13 | async-start | bytes 3784704 | tf_op jit(solution)/shard_map/all_gather | solution.py:228
  7.9 284.1 %all-gather.27.cloned.1.call-start = ((), (), s32[]{:S(2)}) async-start(), calls=%async_computation.18 | async-start | bytes 2162688 | tf_op jit(solution)/shard_map/all_gather | solution.py:234
  8.7 296.7 %all-gather.25.cloned.1.call-start = ((), (), s32[]{:S(2)}) async-start(), calls=%async_computation.17 | async-start | bytes 1310720 | tf_op jit(solution)/shard_map/all_gather | solution.py:293
  54.3 46.9 %copy-start.80 = (f32[1024]{0:T(1024)}, f32[1024]{0:T(1024)S(1)}, u32[]{:S(2)}) copy-start(f32[1024]{0:T(1024)S(1)} %convert_element_type.294) | copy-start | bytes 12292
  100.4 198.9 %copy-start.46 = (f32[256,64]{0,1:T(8,128)}, f32[256,64]{0,1:T(8,128)S(1)}, u32[]{:S(2)}) copy-start(f32[256,64]{0,1:T(8,128)S(1)} %get-tuple-element.428) | copy-start | bytes 196612
  100.7 130.2 %copy-start.5 = (bf16[2,256,1024]{2,1,0:T(8,128)(2,1)}, bf16[2,256,1024]{2,1,0:T(8,128)(2,1)S(1)}, u32[]{:S(2)}) copy-start(bf16[2,256,1024]{2,1,0:T(8,128)(2,1)S(1)} %fusion.75) | copy-start | bytes 3145732
  102.0 82.5 %copy-start.113 = (f32[24]{0:T(128)S(1)}, f32[24]{0:T(128)}, u32[]{:S(2)}) copy-start(f32[24]{0:T(128)} %param.37) | copy-start | bytes 292
  102.1 82.5 %copy-start.107 = (f32[24]{0:T(128)S(1)}, f32[24]{0:T(128)}, u32[]{:S(2)}) copy-start(f32[24]{0:T(128)} %param.38) | copy-start | bytes 292
  102.1 223.9 %all-gather.23.cloned.1.call-start = ((), (), s32[]{:S(2)}) async-start(), calls=%async_computation.16 | async-start | bytes 1310720 | tf_op jit(solution)/shard_map/all_gather | solution.py:294
  141.8 47.9 %copy-start.112 = (bf16[4,56]{1,0:T(4,128)(2,1)S(1)}, bf16[4,56]{1,0:T(4,128)(2,1)}, u32[]{:S(2)}) copy-start(bf16[4,56]{1,0:T(4,128)(2,1)} %param.35) | copy-start | bytes 1348
  141.9 200.5 %all-gather.29.cloned.1.call-start = ((), (), s32[]{:S(2)}) async-start(), calls=%async_computation.19 | async-start | bytes 2162688 | tf_op jit(solution)/shard_map/all_gather | solution.py:237
  142.0 84.8 %collective-permute-start = (f32[2,3]{1,0:T(2,128)S(1)}, f32[2,3]{1,0:T(2,128)S(1)}, u32[]{:S(2)}, u32[]{:S(2)}) collective-permute-start(f32[2,3]{1,0:T(2,128)S(1)} %slice.207), channel_id=1, source_target_pairs={{0,1},{1,2},{2,3},{4,5},{5,6},{6,7},{8,9},{9,10},{10,11},{12,13},{... | collective-permute-start | bytes 80 | tf_op jit(solution)/shard_map/ppermute | solution.py:24
  144.3 205.0 %all-gather.37.cloned.1.call-start = ((), (), s32[]{:S(2)}) async-start(), calls=%async_computation.35 | async-start | bytes 3932160 | tf_op jit(solution)/shard_map/all_gather | solution.py:30
  184.5 50.5 %copy-start.33 = (f32[2,256,24]{2,0,1:T(2,128)}, f32[2,256,24]{2,0,1:T(2,128)S(1)}, u32[]{:S(2)}) copy-start(f32[2,256,24]{2,0,1:T(2,128)S(1)} %copy.264) | copy-start | bytes 147460
  184.5 50.5 %copy-start.109 = (f32[24]{0:T(128)}, f32[24]{0:T(128)S(1)}, u32[]{:S(2)}) copy-start(f32[24]{0:T(128)S(1)} %exponential_negate_fusion) | copy-start | bytes 292
  185.2 49.9 %copy-start.26 = (f32[2,256,24]{2,0,1:T(2,128)}, f32[2,256,24]{2,0,1:T(2,128)S(1)}, u32[]{:S(2)}) copy-start(f32[2,256,24]{2,0,1:T(2,128)S(1)} %get-tuple-element.371) | copy-start | bytes 147460
  187.7 79.7 %copy-start.20 = (f32[2,24,2,128]{1,0,3,2:T(2,128)}, f32[2,24,2,128]{1,0,3,2:T(2,128)S(1)}, u32[]{:S(2)}) copy-start(f32[2,24,2,128]{1,0,3,2:T(2,128)S(1)} %copy.285) | copy-start | bytes 147460
  189.6 50.7 %copy-start.92 = (pred[2,256]{1,0:T(4,128)(4,1)}, pred[2,256]{1,0:T(4,128)(4,1)S(1)}, u32[]{:S(2)}) copy-start(pred[2,256]{1,0:T(4,128)(4,1)S(1)} %get-tuple-element.423) | copy-start | bytes 1540
  237.0 3.3 collective-permute-start.1
  263.8 139.2 %all-gather.19.cloned.1.call-start = ((), (), s32[]{:S(2)}) async-start(), calls=%async_computation.14 | async-start | bytes 3244032 | tf_op jit(solution)/shard_map/all_gather | solution.py:227
  264.6 150.3 %all-gather.21.cloned.1.call-start = ((), (), s32[]{:S(2)}) async-start(), calls=%async_computation.15 | async-start | bytes 3244032 | tf_op jit(solution)/shard_map/all_gather | solution.py:233
  265.3 213.3 %all-gather.31.cloned.1.call-start = ((), (), s32[]{:S(2)}) async-start(), calls=%async_computation.20 | async-start | bytes 4325376 | tf_op jit(solution)/shard_map/all_gather | solution.py:239
  266.1 275.9 %all-gather.33.cloned.1.call-start = ((), (), s32[]{:S(2)}) async-start(), calls=%async_computation.21 | async-start | bytes 4325376 | tf_op jit(solution)/shard_map/all_gather | solution.py:240
  266.7 338.7 %all-gather.35.cloned.1.call-start = ((), (), s32[]{:S(2)}) async-start(), calls=%async_computation.22 | async-start | bytes 4325376 | tf_op jit(solution)/shard_map/all_gather | solution.py:241
  267.4 467.1 %reduce-scatter.17.cloned.1.call-start = ((), (), s32[]{:S(2)}) async-start(), calls=%async_computation.23 | async-start | bytes 1310720 | tf_op jit(solution)/shard_map/reduce_scatter | solution.py:382
  282.1 360.0 %copy-start.9 = (pred[2,256,1024]{1,2,0:T(8,128)(4,1)}, pred[2,256,1024]{1,2,0:T(8,128)(4,1)S(1)}, u32[]{:S(2)}) copy-start(pred[2,256,1024]{1,2,0:T(8,128)(4,1)S(1)} %compare_and_fusion) | copy-start | bytes 1572868
  290.3 71.5 %copy-start.60 = (f32[2,256,24]{1,2,0:T(8,128)}, f32[2,256,24]{1,2,0:T(8,128)S(1)}, u32[]{:S(2)}) copy-start(f32[2,256,24]{1,2,0:T(8,128)S(1)} %copy.289) | copy-start | bytes 147460
  419.8 202.4 %copy-start.87 = (f32[512]{0:T(512)}, f32[512]{0:T(512)S(1)}, u32[]{:S(2)}) copy-start(f32[512]{0:T(512)S(1)} %fusion.168) | copy-start | bytes 6148
  421.4 57.2 %copy-start.55 = (bf16[512,1024]{1,0:T(8,128)(2,1)}, bf16[512,1024]{1,0:T(8,128)(2,1)S(1)}, u32[]{:S(2)}) copy-start(bf16[512,1024]{1,0:T(8,128)(2,1)S(1)} %multiply_convert_fusion.3) | copy-start | bytes 3145732
  485.1 120.3 %copy-start.32 = (bf16[2,256,1024]{2,1,0:T(8,128)(2,1)S(1)}, bf16[2,256,1024]{2,1,0:T(8,128)(2,1)}, u32[]{:S(2)}) copy-start(bf16[2,256,1024]{2,1,0:T(8,128)(2,1)} %param.50) | copy-start | bytes 3145732
  661.9 76.3 %all-gather.39.cloned.1.call-start = ((), (), s32[]{:S(2)}) async-start(), calls=%async_computation.36 | async-start | bytes 3932160 | tf_op jit(solution)/shard_map/all_gather | solution.py:53
  682.0 104.2 %reduce-scatter.19.cloned.1.call-start = ((), (), s32[]{:S(2)}) async-start(), calls=%async_computation.24 | async-start | bytes 1310720 | tf_op jit(solution)/shard_map/reduce_scatter | solution.py:385
  734.5 264.2 %reduce-scatter.41.cloned.1.call-start = ((), (), s32[]{:S(2)}) async-start(), calls=%async_computation.37 | async-start | bytes 540672
  783.4 266.4 %reduce-scatter.29.cloned.1.call-start = ((), (), s32[]{:S(2)}) async-start(), calls=%async_computation.29 | async-start | bytes 1081344 | tf_op jit(solution)/shard_map/reduce_scatter | solution.py:496
  786.2 397.0 %reduce-scatter.31.cloned.1.call-start = ((), (), s32[]{:S(2)}) async-start(), calls=%async_computation.30 | async-start | bytes 1081344 | tf_op jit(solution)/shard_map/reduce_scatter | solution.py:497
  790.8 510.0 %reduce-scatter.25.cloned.1.call-start = ((), (), s32[]{:S(2)}) async-start(), calls=%async_computation.27 | async-start | bytes 6488064 | tf_op jit(solution)/shard_map/reduce_scatter | solution.py:494
  797.3 623.5 %reduce-scatter.21.cloned.1.call-start = ((), (), s32[]{:S(2)}) async-start(), calls=%async_computation.25 | async-start | bytes 6488064 | tf_op jit(solution)/shard_map/reduce_scatter | solution.py:488
  803.5 760.2 %reduce-scatter.27.cloned.1.call-start = ((), (), s32[]{:S(2)}) async-start(), calls=%async_computation.28 | async-start | bytes 4325376 | tf_op jit(solution)/shard_map/reduce_scatter | solution.py:495
  817.2 886.3 %reduce-scatter.33.cloned.1.call-start = ((), (), s32[]{:S(2)}) async-start(), calls=%async_computation.31 | async-start | bytes 4325376 | tf_op jit(solution)/shard_map/reduce_scatter | solution.py:498
  822.1 1028.9 %reduce-scatter.35.cloned.1.call-start = ((), (), s32[]{:S(2)}) async-start(), calls=%async_computation.32 | async-start | bytes 8650752 | tf_op jit(solution)/shard_map/reduce_scatter | solution.py:500
  829.7 1168.9 %reduce-scatter.37.cloned.1.call-start = ((), (), s32[]{:S(2)}) async-start(), calls=%async_computation.33 | async-start | bytes 8650752 | tf_op jit(solution)/shard_map/reduce_scatter | solution.py:501
  837.3 1308.7 %reduce-scatter.39.cloned.1.call-start = ((), (), s32[]{:S(2)}) async-start(), calls=%async_computation.34 | async-start | bytes 8650752 | tf_op jit(solution)/shard_map/reduce_scatter | solution.py:502
  845.1 1446.5 %reduce-scatter.23.cloned.1.call-start = ((), (), s32[]{:S(2)}) async-start(), calls=%async_computation.26 | async-start | bytes 7569408 | tf_op jit(solution)/shard_map/reduce_scatter | solution.py:489
  914.7 3.7 collective-permute-start.2
  945.9 47.9 %copy-start.79 = (f32[1024]{0:T(1024)S(1)}, f32[1024]{0:T(1024)}, u32[]{:S(2)}) copy-start(f32[1024]{0:T(1024)} %convert_element_type.313) | copy-start | bytes 12292
  945.9 47.9 %copy-start.88 = (f32[512]{0:T(512)S(1)}, f32[512]{0:T(512)}, u32[]{:S(2)}) copy-start(f32[512]{0:T(512)} %copy-done.87) | copy-start | bytes 6148
  945.9 47.9 %copy-start.91 = (f32[512]{0:T(512)S(1)}, f32[512]{0:T(512)}, u32[]{:S(2)}) copy-start(f32[512]{0:T(512)} %copy-done.90) | copy-start | bytes 6148
  (106 other events, 854.4 us)
Sparse Core Ops, SparseCore 0:
  10.9 64.6 all-gather.16
  78.4 55.4 all-gather.26
  136.1 15.6 all-gather.24
  153.8 16.9 all-gather.22
  173.5 56.5 all-gather.28
  264.0 28.3 all-gather.36
  295.2 58.9 all-gather.18
  357.1 57.7 all-gather.20
  417.7 60.8 all-gather.30
  481.3 60.5 all-gather.32
  544.8 60.5 all-gather.34
  662.0 23.4 reduce-scatter.16
  687.1 28.5 all-gather.38
  734.6 23.3 reduce-scatter.18
  783.5 132.5 reduce-scatter.40
  918.8 130.8 reduce-scatter.28
  1052.4 130.6 reduce-scatter.30
  1190.1 110.5 reduce-scatter.24
  1306.9 113.7 reduce-scatter.20
  1423.6 140.1 reduce-scatter.26
  1566.7 136.8 reduce-scatter.32
  1706.5 144.4 reduce-scatter.34
  1854.0 144.5 reduce-scatter.36
  2001.5 144.5 reduce-scatter.38
  2149.1 142.5 reduce-scatter.22
where the time goes:
time: 2310 us; the launch traced here: 2300 us
  waiting for transfers between devices  1470 us (64%)
  matrix products  306 us (13%)
  blocking collectives  254 us (11%)
  other arithmetic  143 us (6%)
  local copies, waits for them, and re-layouts  102 us (4%)
    reduce_scatter x1, waiting for transfers between devices, body(): lax.psum_scatter(grad_feed_up, ('dp', 'ctx'), scatter_dimension=0, tiled=...  148 us
    reduce_scatter x1, waiting for transfers between devices, body(): lax.psum_scatter(grad_feed_gate, ('dp', 'ctx'), scatter_dimension=0, tile...  147 us
    reduce_scatter x1, waiting for transfers between devices, body(): lax.psum_scatter(grad_feed_down, ('dp', 'ctx'), scatter_dimension=0, tile...  147 us
    reduce_scatter x1, waiting for transfers between devices, body(): lax.psum_scatter(grad_mix_proj, ('dp', 'ctx'), scatter_dimension=0, tiled...  146 us
    reduce_scatter x1, waiting for transfers between devices, body(): lax.psum_scatter(grad_query_proj, ('dp', 'ctx'), scatter_dimension=0, til...  143 us
    reduce_scatter x1, waiting for transfers between devices, body(): lax.psum_scatter(grad_attn_proj, ('dp', 'ctx'), scatter_dimension=0, tile...  140 us
    reduce_scatter x1, waiting for transfers between devices, body(): lax.psum_scatter(grad_value_proj, ('dp', 'ctx'), scatter_dimension=0, til...  133 us
    reduce_scatter x1, waiting for transfers between devices, body(): lax.psum_scatter(grad_gate_proj, ('dp', 'ctx'), scatter_dimension=0, tile...  120 us
  transfers between devices with their start and end apart: 28, of which 14 were waited for; matrix products, arithmetic and copies ran while one was open for 21% of the time, Pallas kernels for 0%

commit v1 on v0

v1 whole, which is shorter than its diff:
```python
import jax
import jax.numpy as jnp
from jax import lax
from jax.sharding import PartitionSpec as P

MH = 24
MP = 64
DS = 128
KC = 4
QH = 8
KVH = 2
HD = 128


epsilon = 1e-05
highest = lax.Precision.HIGHEST
rope_base = 100000000000.0
masked_score = -1e30


def shifted(block, axis, distance):
    devices = range(lax.axis_size(axis))
    route = [(i - distance, i) for i in devices if i - distance in devices]
    return lax.ppermute(block, axis, route)


def index_bits(axis):
    size = lax.axis_size(axis)
    return [(axis, 1 << k) for k in range(size.bit_length() - 1)]


def bit_weight(bit):
    return bit[1] * (lax.axis_size("ctx") if bit[0] == "dp" else 1)


def bit_value(bit):
    return lax.rem(lax.axis_index(bit[0]) // bit[1], 2)


def exchanged(block, bit):
    route = [(i, i ^ bit[1]) for i in range(lax.axis_size(bit[0]))]
    return lax.ppermute(block, bit[0], route)


def halving_order(first_dp):
    ctx_bits, dp_bits = index_bits("ctx"), index_bits("dp")
    if first_dp:
        return ctx_bits[:1] + dp_bits[:1] + ctx_bits[1:] + dp_bits[1:]
    return ctx_bits + dp_bits


def grown(block, order):
    seen = []
    for bit in reversed(order):
        place = sum(bit_weight(b) > bit_weight(bit) for b in seen)
        other = exchanged(block, bit)
        low_half = bit_value(bit) == 0
        block = jnp.stack(
            [jnp.where(low_half, block, other), jnp.where(low_half, other, block)], axis=place
        )
        seen.append(bit)
    return block.reshape((-1,) + block.shape[len(seen) :])


def shrunk(blocks, order):
    left = list(order)
    total = blocks.reshape((2,) * len(left) + blocks.shape[1:])
    for bit in order:
        place = sum(bit_weight(b) > bit_weight(bit) for b in left)
        here = bit_value(bit)
        away = lax.dynamic_index_in_dim(total, 1 - here, place, keepdims=False)
        keep = lax.dynamic_index_in_dim(total, here, place, keepdims=False)
        added = keep.astype(jnp.float32) + exchanged(away, bit).astype(jnp.float32)
        left.remove(bit)
        total = added.astype(jnp.bfloat16) if left else added
    return total


def gather_rows(shard, first_dp):
    return grown(shard, halving_order(first_dp))


def scatter_rows(partial, rows, first_dp):
    return shrunk(partial.reshape((-1, rows) + partial.shape[1:]), halving_order(first_dp))


def butterfly_sum(value):
    for bit in halving_order(False):
        value = value + exchanged(value, bit)
    return value


def prefix(value, axis, combine, identity):
    size, here = (lax.axis_size(axis), lax.axis_index(axis))
    everything = jax.tree.map(
        lambda part, kind: lax.all_gather(part.astype(kind), axis),
        value,
        (jnp.bfloat16, jnp.bfloat16),
    )
    start = jax.tree.map(
        lambda part, zero: jnp.broadcast_to(jnp.asarray(zero, part.dtype), part.shape),
        value,
        identity,
    )

    def prefix_hop(k, before):
        reached = k < here
        new = combine(
            before, jax.tree.map(lambda part, own: part[k].astype(own.dtype), everything, value)
        )
        return jax.tree.map(lambda a, b: jnp.where(reached, a, b), new, before)

    return lax.fori_loop(0, size, prefix_hop, start)


def entering(value, axis, combine, identity):
    size, here = (lax.axis_size(axis), lax.axis_index(axis))
    everything = jax.tree.map(
        lambda part, kind: lax.all_gather(part.astype(kind), axis),
        value,
        jax.tree.map(lambda a: jnp.bfloat16 if a.dtype == jnp.float32 else a.dtype, value),
    )
    start = jax.tree.map(
        lambda part, zero: jnp.broadcast_to(jnp.asarray(zero, part.dtype), part.shape),
        value,
        identity,
    )

    def entering_hop(k, before):
        at = size - 1 - k
        reached = at > here
        new = combine(
            before, jax.tree.map(lambda part, own: part[at].astype(own.dtype), everything, value)
        )
        return jax.tree.map(lambda a, b: jnp.where(reached, a, b), new, before)

    return lax.fori_loop(0, size, entering_hop, start)


def rms_scale(features):
    return lax.rsqrt(jnp.mean(features * features, axis=-1, keepdims=True) + epsilon)


def gained_norm(features, gain_vec):
    return features * rms_scale(features) * gain_vec


def forward_mul(left, right):
    return jnp.dot(left, right, preferred_element_type=jnp.float32)


def outer_sum(left, right):
    return lax.dot_general(
        left, right, (((0,), (0,)), ((), ())), preferred_element_type=jnp.float32
    )


def back_mul(grad_rows, weight):
    return lax.dot_general(
        grad_rows, weight, (((1,), (1,)), ((), ())), preferred_element_type=jnp.float32
    )


def rotate(features, positions, direction):
    head_size = features.shape[-1]
    half_size = head_size // 2
    freq_exp = lax.broadcasted_iota(jnp.int32, (half_size,), 0).astype(positions.dtype) * (
        2.0 / head_size
    )
    inverse = jnp.power(rope_base, -freq_exp)
    angles = positions[:, None] * inverse[None, :]
    cosine = jnp.cos(angles)[:, None, :]
    sine_part = direction * jnp.sin(angles)[:, None, :]
    first_half = features[..., :half_size]
    second_half = features[..., half_size:]
    return jnp.concatenate(
        [
            first_half * cosine - second_half * sine_part,
            second_half * cosine + first_half * sine_part,
        ],
        axis=-1,
    )


def conv_local(extended, segment_wide, conv_taps, conv_bias):
    tap_count = conv_taps.shape[0]
    length_now = extended.shape[1] - tap_count + 1
    segment_now = segment_wide[:, tap_count - 1 :]
    conv_total = conv_bias
    for offset in range(tap_count):
        window = extended[:, offset : offset + length_now]
        same_doc = (segment_wide[:, offset : offset + length_now] == segment_now)[..., None]
        conv_total = conv_total + conv_taps[offset] * jnp.where(same_doc, window, 0.0)
    return conv_total


def prepare(extended, segment_wide, step_raw, conv_taps, conv_bias, step_bias, decay_log):
    activated = jax.nn.silu(conv_local(extended, segment_wide, conv_taps, conv_bias))
    inner_width = MH * MP
    inner_vals = activated[..., :inner_width].reshape(activated.shape[:-1] + (MH, MP))
    input_map = activated[..., inner_width : inner_width + DS]
    output_map = activated[..., inner_width + DS :]
    step_size = jax.nn.softplus(step_raw + step_bias)
    log_decay = -jnp.exp(decay_log) * step_size
    return (inner_vals, input_map, output_map, step_size, log_decay)


def block_output(
    step_size, log_decay, inner_vals, input_map, output_map, segment_ids, start_flag, state_in
):
    count_rows = log_decay.shape[0]
    cumulative = jnp.cumsum(log_decay, axis=0)
    carried = (jnp.cumsum(start_flag) == 0).astype(cumulative.dtype)
    row_index = lax.broadcasted_iota(jnp.int32, (count_rows, count_rows), 0)
    col_index = lax.broadcasted_iota(jnp.int32, (count_rows, count_rows), 1)
    allowed = ((col_index <= row_index) & (segment_ids[:, None] == segment_ids[None, :]))[
        :, :, None
    ]
    spread = cumulative[:, None, :] - cumulative[None, :, :]
    mixing = jnp.where(allowed, jnp.exp(jnp.where(allowed, spread, 0.0)), 0.0)
    affinity = jnp.dot(output_map, input_map.T, precision=highest)
    kernel = affinity[:, :, None] * mixing * step_size[None, :, :]
    result = jnp.einsum("ijh,jhp->ihp", kernel, inner_vals, precision=highest)
    entry_scale = carried[:, None] * jnp.exp(cumulative)
    carried_in = jnp.einsum("is,hps->ihp", output_map, state_in, precision=highest)
    return result + entry_scale[:, :, None] * carried_in


def block_summary(step_size, log_decay, inner_vals, input_map, segment_ids, start_flag):
    cumulative = jnp.cumsum(log_decay, axis=0)
    last_cum = cumulative[-1]
    keep_last = (jnp.sum(start_flag) == 0).astype(cumulative.dtype)
    block_decay = keep_last * jnp.exp(last_cum)
    same_last = (segment_ids == segment_ids[-1])[:, None]
    final_weight = jnp.where(same_last, jnp.exp(last_cum[None, :] - cumulative), 0.0) * step_size
    local_state = jnp.einsum(
        "jh,jhp,js->hps", final_weight, inner_vals, input_map, precision=highest
    )
    return (block_decay, local_state)


def mamba_tail(result, inner_vals, gate_mamba, skip_scale, inner_gain):
    full_out = result + skip_scale[:, None] * inner_vals
    gated_out = full_out.reshape(full_out.shape[:-2] + (MH * MP,)) * jax.nn.silu(gate_mamba)
    return gained_norm(gated_out, inner_gain)


def chain_combine(earlier, later):
    return (earlier[0] * later[0], later[0][..., None, None] * earlier[1] + later[1])


def attention_mask(positions, segment_ids, segment_all):
    key_count = segment_all.shape[1]
    key_pos = lax.broadcasted_iota(jnp.int32, (key_count,), 0).astype(jnp.float32)
    causal = key_pos[None, :] <= positions[:, None]
    same_doc = segment_ids[:, :, None] == segment_all[:, None, :]
    return (causal[None] & same_doc)[:, None, None]


def score_block(grouped, keys_all, allowed):
    scores = jnp.einsum(
        "sikgd,sjkd->skgij", grouped, keys_all, preferred_element_type=jnp.float32
    ) * HD ** (-0.5)
    return jnp.where(allowed, scores, masked_score)


def body(
    tokens,
    segments,
    pre_gain,
    gate_proj,
    mix_proj,
    step_proj,
    conv_taps,
    conv_bias,
    decay_log,
    step_bias,
    skip_scale,
    inner_gain,
    mamba_proj,
    query_proj,
    key_proj,
    value_proj,
    attn_proj,
    feed_gain,
    feed_gate,
    feed_up,
    feed_down,
    cotangent,
):
    shard_rows = gate_proj.shape[0]
    inner_rows = mamba_proj.shape[0]
    attn_rows = attn_proj.shape[0]
    feat_rows = conv_bias.shape[0]
    down_rows = feed_down.shape[0]
    small_parts = (pre_gain, feed_gain, inner_gain, conv_bias, conv_taps.reshape(-1))
    small = jnp.concatenate(small_parts)
    small = jnp.pad(small, (0, shard_rows * 16 - small.shape[0])).reshape(shard_rows, 16)
    step_block = jnp.pad(jnp.concatenate([step_proj, small], axis=1), ((0, 0), (0, 128 - MH - 16)))
    pack_two = gather_rows(
        jnp.concatenate([mix_proj, key_proj, value_proj, step_block], axis=1), True
    ).reshape(-1, 2304 + 128)
    pack_one = gather_rows(jnp.concatenate([gate_proj, query_proj], axis=1), False).reshape(
        -1, 2560
    )
    pack_mix = gather_rows(jnp.concatenate([mamba_proj, attn_proj], axis=0), True)
    mamba_whole = pack_mix[:, :inner_rows].reshape(-1, pack_mix.shape[-1])
    attn_whole = pack_mix[:, inner_rows:].reshape(-1, pack_mix.shape[-1])
    gate_whole = gather_rows(feed_gate, False).reshape(-1, feed_gate.shape[1])
    up_whole = gather_rows(feed_up, True).reshape(-1, feed_up.shape[1])
    down_whole = gather_rows(feed_down, False).reshape(-1, feed_down.shape[1])
    small_all = pack_two[:, 2304 + MH : 2304 + MH + 16].reshape(-1, shard_rows * 16)
    cuts = [0]
    for part in small_parts:
        cuts.append(cuts[-1] + part.shape[0])
    pre_whole, feed_whole, inner_whole, bias_whole = (
        small_all[:, cuts[k] : cuts[k + 1]].reshape(-1).astype(jnp.float32) for k in range(4)
    )
    taps_float = (
        small_all[:, cuts[4] : cuts[5]]
        .reshape(-1, KC, feat_rows)
        .transpose(1, 0, 2)
        .reshape(KC, -1)
        .astype(jnp.float32)
    )
    seq_count, block_rows, model_width = tokens.shape
    tap_count = KC
    inner_width = MH * MP
    group_size = QH // KVH
    ctx_index = lax.axis_index("ctx")
    flat_rows = tokens.reshape(seq_count * block_rows, model_width).astype(jnp.float32)
    normed = gained_norm(flat_rows, pre_whole).astype(jnp.bfloat16)
    front_one = forward_mul(normed, pack_one)
    front_two = forward_mul(normed, pack_two)
    gate_mamba = front_one[:, :inner_width].reshape(seq_count, block_rows, inner_width)
    conv_input = front_two[:, :1792].reshape(seq_count, block_rows, -1)
    step_raw = front_two[:, 2304 : 2304 + MH].reshape(seq_count, block_rows, MH)
    segment_ids = segments.astype(jnp.float32)
    prev_rows, prev_segment = shifted(
        (conv_input[:, block_rows - tap_count + 1 :], segment_ids[:, block_rows - tap_count + 1 :]),
        "ctx",
        1,
    )
    extended = jnp.concatenate([prev_rows, conv_input], axis=1)
    segment_wide = jnp.concatenate([prev_segment, segment_ids], axis=1)
    start_flag = (
        segment_ids != segment_wide[:, tap_count - 2 : tap_count - 2 + block_rows]
    ).astype(jnp.float32)
    prepared, prepare_back = jax.vjp(
        lambda *rest: prepare(rest[0], segment_wide, *rest[1:]),
        extended,
        step_raw,
        taps_float,
        bias_whole,
        step_bias,
        decay_log,
    )
    inner_vals, input_map, output_map, step_size, log_decay = prepared
    (block_decay, local_state), summary_back = jax.vjp(
        lambda step_in, log_in, inner_in, input_in: jax.vmap(block_summary)(
            step_in, log_in, inner_in, input_in, segment_ids, start_flag
        ),
        step_size,
        log_decay,
        inner_vals,
        input_map,
    )
    identity_pair = (jnp.ones_like(block_decay), jnp.zeros_like(local_state))
    carried = prefix((block_decay, local_state), "ctx", chain_combine, identity_pair)
    state_in = carried[1]
    def mamba_front(step_in, log_in, inner_in, input_in, output_in, state_arg, gate_in, skip_in, gain_in):
        result_in = jax.vmap(block_output)(
            step_in, log_in, inner_in, input_in, output_in, segment_ids, start_flag, state_arg
        )
        return mamba_tail(result_in, inner_in, gate_in, skip_in, gain_in)

    mixed, front_back = jax.vjp(
        mamba_front,
        step_size,
        log_decay,
        inner_vals,
        input_map,
        output_map,
        state_in,
        gate_mamba,
        skip_scale,
        inner_whole,
    )
    mixed_low = mixed.astype(jnp.bfloat16)
    branch_mamba = forward_mul(mixed_low.reshape(-1, inner_width), mamba_whole)
    positions = (ctx_index * block_rows + lax.broadcasted_iota(jnp.int32, (block_rows,), 0)).astype(
        jnp.float32
    )
    query_pre = front_one[:, inner_width:].reshape(seq_count, block_rows, QH, HD)
    key_pre = front_two[:, 1792:2048].reshape(seq_count, block_rows, KVH, HD)
    value_pre = front_two[:, 2048:2304].reshape(seq_count, block_rows, KVH, HD)
    queries = rotate(query_pre, positions, 1.0).astype(jnp.bfloat16)
    keys_rot = rotate(key_pre, positions, 1.0).astype(jnp.bfloat16)
    values = value_pre.astype(jnp.bfloat16)
    ctx_size = lax.axis_size("ctx")
    ctx_order = index_bits("ctx")
    both = grown(jnp.concatenate([keys_rot, values], axis=2), ctx_order)
    both = both.transpose(1, 0, 2, 3, 4).reshape(seq_count, -1, 2 * KVH, HD)
    keys_all, values_all = both[:, :, :KVH], both[:, :, KVH:]
    segment_all = grown(segment_ids.astype(jnp.bfloat16), ctx_order)
    segment_all = segment_all.transpose(1, 0, 2).reshape(seq_count, -1)
    grouped = queries.reshape(seq_count, block_rows, KVH, group_size, HD)
    allowed = attention_mask(positions, segment_ids, segment_all.astype(jnp.float32))
    scores = score_block(grouped, keys_all, allowed)
    row_max = jnp.max(scores, axis=-1, keepdims=True)
    log_total = row_max + jnp.log(jnp.sum(jnp.exp(scores - row_max), axis=-1, keepdims=True))
    attend = jnp.exp(scores - log_total).astype(jnp.bfloat16)
    attended = jnp.einsum(
        "skgij,sjkd->sikgd", attend, values_all, preferred_element_type=jnp.float32
    ).astype(jnp.bfloat16)
    branch_attn = forward_mul(attended.reshape(-1, QH * HD), attn_whole)
    residual = flat_rows + branch_mamba + branch_attn
    feed_scale = feed_whole
    normed_two = gained_norm(residual, feed_scale).astype(jnp.bfloat16)
    feed_gate_out = forward_mul(normed_two, gate_whole)
    feed_up_out = forward_mul(normed_two, up_whole)
    feed_hidden = (jax.nn.silu(feed_gate_out) * feed_up_out).astype(jnp.bfloat16)
    output = (
        (residual + forward_mul(feed_hidden, down_whole))
        .astype(jnp.bfloat16)
        .reshape(seq_count, block_rows, model_width)
    )
    upstream = cotangent.reshape(-1, model_width)
    grad_feed_down = outer_sum(feed_hidden, upstream)
    grad_hidden = back_mul(upstream, down_whole)
    _, swiglu_back = jax.vjp(
        lambda gate_arg, up_arg: jax.nn.silu(gate_arg) * up_arg, feed_gate_out, feed_up_out
    )
    grad_gate_ff, grad_up_ff = swiglu_back(grad_hidden)
    gate_ff_low = grad_gate_ff.astype(jnp.bfloat16)
    up_ff_low = grad_up_ff.astype(jnp.bfloat16)
    grad_feed_gate = outer_sum(normed_two, gate_ff_low)
    grad_feed_up = outer_sum(normed_two, up_ff_low)
    grad_normed_two = back_mul(gate_ff_low, gate_whole) + back_mul(
        up_ff_low, up_whole
    )
    _, norm_two_back = jax.vjp(gained_norm, residual, feed_whole)
    grad_res_norm, grad_feed_gain = norm_two_back(grad_normed_two)
    grad_residual = upstream.astype(jnp.float32) + grad_res_norm
    residual_low = grad_residual.astype(jnp.bfloat16)
    grad_mamba_proj = outer_sum(mixed_low.reshape(-1, inner_width), residual_low)
    grad_attn_proj = outer_sum(attended.reshape(-1, QH * HD), residual_low)
    grad_mixed = back_mul(residual_low, mamba_whole).reshape(
        seq_count, block_rows, inner_width
    )
    grad_attended = (
        back_mul(residual_low, attn_whole)
        .astype(jnp.bfloat16)
        .reshape(seq_count, block_rows, KVH, group_size, HD)
    )
    scores_again = score_block(grouped, keys_all, allowed)
    attend_full = jnp.exp(scores_again - log_total)
    attend_again = attend_full.astype(jnp.bfloat16)
    grad_attend = jnp.einsum(
        "sikgd,sjkd->skgij", grad_attended, values_all, preferred_element_type=jnp.float32
    )
    grad_values_all = jnp.einsum(
        "skgij,sikgd->sjkd", attend_again, grad_attended, preferred_element_type=jnp.float32
    )
    row_dot = jnp.sum(attend_full * grad_attend, axis=-1, keepdims=True)
    grad_scores = (attend_full * (grad_attend - row_dot)).astype(jnp.bfloat16)
    grad_queries = jnp.einsum(
        "skgij,sjkd->sikgd", grad_scores, keys_all, preferred_element_type=jnp.float32
    ) * HD ** (-0.5)
    grad_keys_all = jnp.einsum(
        "skgij,sikgd->sjkd", grad_scores, grouped, preferred_element_type=jnp.float32
    ) * HD ** (-0.5)
    grad_both = jnp.concatenate([grad_keys_all, grad_values_all], axis=2).astype(jnp.bfloat16)
    grad_both = grad_both.reshape(seq_count, ctx_size, block_rows, 2 * KVH, HD)
    grad_both = shrunk(grad_both.transpose(1, 0, 2, 3, 4), ctx_order)
    grad_keys, grad_values = grad_both[:, :, :KVH], grad_both[:, :, KVH:]
    query_low = (
        rotate(grad_queries.reshape(seq_count, block_rows, QH, HD), positions, -1.0)
        .astype(jnp.bfloat16)
        .reshape(-1, QH * HD)
    )
    key_low = rotate(grad_keys, positions, -1.0).astype(jnp.bfloat16).reshape(-1, KVH * HD)
    value_low = grad_values.astype(jnp.bfloat16).reshape(-1, KVH * HD)
    front_grads = front_back(grad_mixed)
    chain_grads = entering((block_decay, front_grads[5]), "ctx", chain_combine, identity_pair)
    grad_state_out = chain_grads[1]
    grad_decay = jnp.sum(grad_state_out * state_in, axis=(2, 3))
    summary_grads = summary_back((grad_decay, grad_state_out))
    (
        grad_extended,
        grad_step_raw,
        grad_conv_taps,
        grad_conv_bias,
        grad_step_bias,
        grad_decay_log,
    ) = prepare_back(
        (
            front_grads[2] + summary_grads[2],
            front_grads[3] + summary_grads[3],
            front_grads[4],
            front_grads[0] + summary_grads[0],
            front_grads[1] + summary_grads[1],
        )
    )
    back_rows = shifted(grad_extended[:, : tap_count - 1].astype(jnp.bfloat16), "ctx", -1).astype(
        jnp.float32
    )
    grad_conv_input = (
        grad_extended[:, tap_count - 1 :].at[:, block_rows - tap_count + 1 :].add(back_rows)
    )
    gate_low = front_grads[6].astype(jnp.bfloat16).reshape(-1, inner_width)
    conv_low = grad_conv_input.astype(jnp.bfloat16).reshape(-1, grad_conv_input.shape[-1])
    step_low = grad_step_raw.astype(jnp.bfloat16).reshape(-1, MH)
    lows_one = jnp.concatenate([gate_low, query_low], axis=1)
    lows_two = jnp.concatenate([conv_low, key_low, value_low], axis=1)
    step_wide = jnp.pad(step_low, ((0, 0), (0, 128 - MH)))
    grad_one = outer_sum(normed, lows_one)
    grad_two = outer_sum(normed, lows_two)
    grad_step = outer_sum(normed, step_low)
    grad_normed = back_mul(lows_one, pack_one) + back_mul(
        jnp.concatenate([lows_two, step_wide], axis=1), pack_two
    )
    _, norm_one_back = jax.vjp(gained_norm, flat_rows, pre_whole)
    grad_flat, grad_pre_gain = norm_one_back(grad_normed)
    grad_tokens = (grad_residual + grad_flat).reshape(seq_count, block_rows, model_width)
    device_count = lax.axis_size("dp") * ctx_size
    small_grads = jnp.concatenate(
        [
            grad_pre_gain.reshape(device_count, -1),
            grad_feed_gain.reshape(device_count, -1),
            front_grads[8].reshape(device_count, -1),
            grad_conv_bias.reshape(device_count, -1),
            grad_conv_taps.reshape(KC, device_count, -1)
            .transpose(1, 0, 2)
            .reshape(device_count, -1),
        ],
        axis=1,
    )
    small_grads = jnp.pad(
        small_grads, ((0, 0), (0, shard_rows * 16 - small_grads.shape[1]))
    ).reshape(-1, 16)
    step_grads = jnp.pad(
        jnp.concatenate([grad_step, small_grads], axis=1), ((0, 0), (0, 128 - MH - 16))
    )
    low = jnp.bfloat16
    own_down = scatter_rows(grad_feed_down.astype(low), down_rows, False)
    own_gate = scatter_rows(grad_feed_gate.astype(low), shard_rows, False)
    own_up = scatter_rows(grad_feed_up.astype(low), shard_rows, True)
    own_mix = scatter_rows(
        jnp.concatenate(
            [
                grad_mamba_proj.astype(low).reshape(device_count, inner_rows, -1),
                grad_attn_proj.astype(low).reshape(device_count, attn_rows, -1),
            ],
            axis=1,
        ).reshape(device_count * (inner_rows + attn_rows), -1),
        inner_rows + attn_rows,
        True,
    )
    own_one = scatter_rows(grad_one.astype(low), shard_rows, False)
    own_two = scatter_rows(
        jnp.concatenate([grad_two.astype(low), step_grads.astype(low)], axis=1), shard_rows, True
    )
    own_small = own_two[:, 2304 + MH : 2304 + MH + 16].reshape(-1)
    head_sums = butterfly_sum(jnp.stack([grad_decay_log, grad_step_bias, front_grads[7]]))
    return (
        output,
        grad_tokens,
        own_small[cuts[0] : cuts[1]],
        own_one[:, :inner_width],
        own_two[:, :1792],
        own_two[:, 2304 : 2304 + MH],
        own_small[cuts[4] : cuts[5]].reshape(KC, feat_rows),
        own_small[cuts[3] : cuts[4]],
        head_sums[0],
        head_sums[1],
        head_sums[2],
        own_small[cuts[2] : cuts[3]],
        own_mix[:inner_rows],
        own_one[:, inner_width:],
        own_two[:, 1792:2048],
        own_two[:, 2048:2304],
        own_mix[inner_rows:],
        own_small[cuts[1] : cuts[2]],
        own_gate,
        own_up,
        own_down,
    )


def solution(mesh):
    return jax.shard_map(
        body,
        mesh=mesh,
        in_specs=(
            P("dp", "ctx", None),
            P("dp", "ctx"),
            P(("dp", "ctx")),
            P(("dp", "ctx"), None),
            P(("dp", "ctx"), None),
            P(("dp", "ctx"), None),
            P(None, ("dp", "ctx")),
            P(("dp", "ctx")),
            P(),
            P(),
            P(),
            P(("dp", "ctx")),
            P(("dp", "ctx"), None),
            P(("dp", "ctx"), None),
            P(("dp", "ctx"), None),
            P(("dp", "ctx"), None),
            P(("dp", "ctx"), None),
            P(("dp", "ctx")),
            P(("dp", "ctx"), None),
            P(("dp", "ctx"), None),
            P(("dp", "ctx"), None),
            P("dp", "ctx", None),
        ),
        out_specs=(
            P("dp", "ctx", None),
            P("dp", "ctx", None),
            P(("dp", "ctx")),
            P(("dp", "ctx"), None),
            P(("dp", "ctx"), None),
            P(("dp", "ctx"), None),
            P(None, ("dp", "ctx")),
            P(("dp", "ctx")),
            P(),
            P(),
            P(),
            P(("dp", "ctx")),
            P(("dp", "ctx"), None),
            P(("dp", "ctx"), None),
            P(("dp", "ctx"), None),
            P(("dp", "ctx"), None),
            P(("dp", "ctx"), None),
            P(("dp", "ctx")),
            P(("dp", "ctx"), None),
            P(("dp", "ctx"), None),
            P(("dp", "ctx"), None),
        ),
        check_vma=False,
    )
```

time: 2310 us -> 968 us (0.42)
  waiting for transfers between devices: 1470 us -> 269 us
  blocking collectives: 254 us -> 5.42 us
  local copies, waits for them, and re-layouts: 102 us -> 177 us
  matrix products: 306 us -> 236 us
  starting transfers between devices: 7.36 us -> 65 us
  other arithmetic: 143 us -> 191 us
    reduce_scatter x12 -> x0, waiting for transfers between devices: 1290 us -> none  [the longest x1 148 us: body(): lax.psum_scatter(grad_feed_up, ('dp', 'ctx'), scatter_dimension=0, tiled=...]
    ppermute x0 -> x71, waiting for transfers between devices: none -> 269 us  [exchanged(): return lax.ppermute(block, bit[0], route)]
    all_gather x10 -> x0, waiting for transfers between devices: 173 us -> none  [the longest x1 57.2 us: body(): lax.all_gather(feed_gate, ('dp', 'ctx'), axis=0, tiled=True)]
    all_gather x5 -> x0, blocking collectives: 164 us -> none  [the longest x1 42.8 us: body(): lax.all_gather(key_proj, ('dp', 'ctx'), axis=0, tiled=True)]
    unnamed x2 -> x0, blocking collectives: 84.6 us -> none
    ppermute x0 -> x71, starting transfers between devices: none -> 59.5 us  [exchanged(): return lax.ppermute(block, bit[0], route)]
    another operation x16 -> x82, other arithmetic: 18 us -> 52.9 us  [the longest x66 32.3 us: grown(): jnp.stack([jnp.where(low_half, block, other), jnp.where(low_half, other,...]
    dot_general x11 -> x8, matrix products: 57.6 us -> 25.8 us  [outer_sum(): lax.dot_general(left, right, (((0,), (0,)), ((), ())), preferred_element_...]
  transfers between devices with their start and end apart: 28 -> 76, of which waited for: 14 -> 37; matrix products, arithmetic and copies ran while one was open for 21% -> 43% of each run, Pallas kernels for 0% -> 0%
where the time goes in v1:
time: 968 us; the launch traced here: 961 us
  waiting for transfers between devices  269 us (28%)
  matrix products  236 us (24%)
  other arithmetic  191 us (20%)
  local copies, waits for them, and re-layouts  177 us (18%)
  starting transfers between devices  65 us (7%)
  between operations  17.7 us (2%)
    ppermute x71, waiting for transfers between devices, exchanged(): return lax.ppermute(block, bit[0], route)  269 us
    ppermute x71, starting transfers between devices, exchanged(): return lax.ppermute(block, bit[0], route)  59.5 us
    dot_general x3, matrix products, block_output(): result = jnp.einsum('ijh,jhp->ihp', kernel, inner_vals, precision=highest)  55.6 us
    unnamed x349, local copies, waits for them, and re-layouts  37.7 us
    another operation x66, other arithmetic, grown(): jnp.stack([jnp.where(low_half, block, other), jnp.where(low_half, other,...  32.3 us
    dot_general x7, matrix products, back_mul(): lax.dot_general(grad_rows, weight, (((1,), (1,)), ((), ())), preferred_el...  29.7 us
    dot_general x7, matrix products, forward_mul(): return jnp.dot(left, right, preferred_element_type=jnp.float32)  28.6 us
    dot_general x8, matrix products, outer_sum(): lax.dot_general(left, right, (((0,), (0,)), ((), ())), preferred_element_...  25.8 us
  transfers between devices with their start and end apart: 76, of which 37 were waited for; matrix products, arithmetic and copies ran while one was open for 43% of the time, Pallas kernels for 0%

profile of v1, /device:TPU:0, one launch (start us, length us, event | category | flops | bytes accessed | tf_op | source)
XLA Modules:
  0.0 961.5 jit_solution(5506382245096562206)
XLA Ops:
  46.6 7.4 collective-permute-done.26
  72.7 5.5 collective-permute-done.22
  79.9 5.0 collective-permute-done.1
  86.6 5.4 collective-permute-done.8
  92.1 6.5 collective-permute-done.13
  109.2 9.1 collective-permute-done.9
  123.2 17.6 %collective-permute-done.29 = bf16[2,2,2,32,2048]{4,3,2,1,0:T(8,128)(2,1)S(1)} collective-permute-done((bf16[2,2,2,32,2048]{4,3,2,1,0:T(8,128)(2,1)S(1)}, bf16[2,2,2,32,2048]{4,3,2,1,0:T(8,128)(2,1)S(1)}, u32[]{:S(2)}, u32[]{:S(2)}) %collective-permute-start.29) | collective-permute-done | bytes 1048608 | tf_op jit(solution)/shard_map/ppermute | solution.py:42
  145.8 22.1 %collective-permute-done.24 = bf16[2,2,2,32,2048]{4,3,0,1,2:T(8,128)(2,1)S(1)} collective-permute-done((bf16[2,2,2,32,2048]{4,3,0,1,2:T(8,128)(2,1)S(1)}, bf16[2,2,2,32,2048]{4,3,0,1,2:T(8,128)(2,1)S(1)}, u32[]{:S(2)}, u32[]{:S(2)}) %collective-permute-start.24) | collective-permute-done | bytes 1048608 | tf_op jit(solution)/shard_map/ppermute | solution.py:42
  169.6 24.6 %collective-permute-done.10 = bf16[2,2,2,32,2560]{4,3,2,1,0:T(8,128)(2,1)S(1)} collective-permute-done((bf16[2,2,2,32,2560]{4,3,2,1,0:T(8,128)(2,1)S(1)}, bf16[2,2,2,32,2560]{4,3,2,1,0:T(8,128)(2,1)S(1)}, u32[]{:S(2)}, u32[]{:S(2)}) %collective-permute-start.10) | collective-permute-done | bytes 1310752 | tf_op jit(solution)/shard_map/ppermute | solution.py:42
  224.8 5.3 fusion.214
  286.6 5.4 all_gather.18
  292.0 11.8 %fusion.50 = (f32[2,256,1792]{2,1,0:T(8,128)S(1)}, f32[2,256,1792]{2,1,0:T(8,128)}) fusion(f32[2,256,1792]{2,1,0:T(8,128)} %bitcast.745, pred[2,256]{1,0:T(4,128)(4,1)} %get-tuple-element.639, f32[1792]{0:T(1024)S(1)} %mul.803, f32[2,3,1792]{2,1,0:T(4,128)} %collective-permute-done.6, pred[2,256]{1,0:T(4,128)(4,1)} %get-tuple-element.629, ...), kind=kLoop, calls=%fused_computation.107 | loop fusion | flops 17432576 | bytes 11090944 | tf_op jit(solution)/shard_map/jvp(jit(silu))/mul | solution.py:198
  311.4 5.7 fusion.111
  342.1 5.7 reshape.952
  347.8 6.2 copy.656
  357.2 7.6 fusion.15
  364.8 9.2 exponential_reduce_fusion
  374.0 11.2 %fusion.117 = bf16[2,256,2,4,128]{1,4,3,2,0:T(8,128)(2,1)} fusion(bf16[2,1024,4,128]{3,1,2,0:T(8,128)(2,1)} %bitcast.754, f32[2,2,1024,256,4]{3,2,4,1,0:T(8,128)} %get-tuple-element.648, f32[2,2,4,256]{3,2,1,0:T(4,128)S(1)} %bitcast.828, pred[2,256,1024]{1,2,0:T(8,128)(4,1)S(1)} %compare_and_fusion), kind=kOutput, calls=%fused_computation.243 | convolution fusion | flops 1091043328 | bytes 19415040 | tf_op jit(solution)/shard_map/skgij,sjkd->sikgd/dot_general | solution.py:413
  393.4 8.8 while.31
  406.6 18.4 %multiply_reduce_fusion.10 = (f32[2,256]{1,0:T(2,128)S(1)}, f32[2,256,24,64]{1,3,2,0:T(8,128)}) fusion(f32[2,256,24,64]{1,3,2,0:T(8,128)} %copy.656, f32[2,256,24,64]{1,3,2,0:T(8,128)S(1)} %bitcast.741, f32[24]{0:T(128)S(1)} %copy-done.151, f32[2,256,24,64]{1,3,2,0:T(8,128)S(1)} %fusion.155, f32[2,256,24]{1,2,0:T(8,128)S(1)} %copy-done.92, ...), kind=kOutput, calls=%fused_computation.126 | convolution fusion | flops 2440297984 | bytes 13387872 | tf_op jit(solution)/shard_map/jvp(vmap(ijh,jhp->ihp))/dot_general | solution.py:223
  425.0 6.0 copy.759
  451.4 5.6 fusion.37
  491.0 11.7 %fusion.119 = bf16[2,1024,2,128]{1,3,2,0:T(8,128)(2,1)} fusion(bf16[2,256,2,4,128]{1,4,3,2,0:T(8,128)(2,1)} %copy.696, f32[2,2,1024,256,4]{3,2,4,1,0:T(8,128)} %get-tuple-element.648, f32[2,2,4,256]{3,2,1,0:T(4,128)S(1)} %bitcast.829, pred[2,256,1024]{1,2,0:T(8,128)(4,1)S(1)} %copy-done.12), kind=kOutput, calls=%fused_computation.245 | convolution fusion | flops 1091043328 | bytes 19415040 | tf_op jit(solution)/shard_map/skgij,sikgd->sjkd/dot_general | solution.py:462
  502.7 13.4 %fusion.2 = (f32[2,2,4,256]{3,2,1,0:T(4,128)S(1)}, f32[2,2,1024,256,4]{3,2,4,1,0:T(8,128)}) fusion(f32[2,2,1024,256,4]{3,2,4,1,0:T(8,128)} %get-tuple-element.648, f32[2,2,4,256]{3,2,1,0:T(4,128)S(1)} %bitcast.830, pred[2,256,1024]{1,2,0:T(8,128)(4,1)S(1)} %copy-done.12, bf16[2,256,2,4,128]{1,4,3,2,0:T(8,128)(2,1)} %copy.696, ...), kind=kOutput, calls=%fused_computation.8 | convolution fusion | flops 1094709248 | bytes 36208640 | tf_op jit(solution)/shard_map/sikgd,sjkd->skgij/dot_general | solution.py:459
  516.1 8.1 fusion.127
  524.2 11.3 %fusion.4 = bf16[2,2,4,256,1024]{3,4,2,1,0:T(8,128)(2,1)} fusion(f32[2,2,1024,256,4]{3,2,4,1,0:T(8,128)} %get-tuple-element.658, f32[2,2,1024,256,4]{3,2,4,1,0:T(8,128)S(1)} %bitcast.732, f32[2,2,4,256]{3,2,1,0:T(4,128)S(1)} %get-tuple-element.657, f32[2,2,4,256]{3,2,1,0:T(4,128)S(1)} %bitcast.831, pred[2,256,1024]{1,2,0:T(8,128)(4,1)S(1)} %copy-done.12), kind=kLoop, calls=%fused_computation.10 | loop fusion | flops 25165824 | bytes 42500096 | tf_op jit(solution)/shard_map/convert_element_type | solution.py:466
  535.5 7.7 fusion.118
  561.3 22.7 %fusion.17 = (f32[2,256,24]{1,2,0:T(8,128)}, f32[2,256,24]{1,2,0:T(8,128)}, f32[2,256,24]{1,2,0:T(8,128)}, f32[2,256,256]{2,1,0:T(8,128)}) fusion(f32[2,256,24]{1,2,0:T(8,128)S(1)} %copy-done.118, f32[2,256,24]{1,2,0:T(8,128)S(1)} %copy-done.119, f32[2,256,256]{2,1,0:T(8,128)} %fusion.160, pred[2,256,256]{2,1,0:T(8,128)(4,1)} %compare_and_fusion.1, ...), kind=kOutput, calls=%fused_computation.30 | convolution fusion | flops 2462937088 | bytes 7716864 | tf_op jit(solution)/shard_map/transpose(jvp(vmap(ijh,jhp->ihp)))/dot_general | solution.py:223
  587.2 5.0 reduce-window.34
  633.4 9.3 collective-permute-done.38
  654.5 18.1 %collective-permute-done.60 = bf16[2,2,2,32,2048]{4,3,0,1,2:T(8,128)(2,1)S(1)} collective-permute-done((bf16[2,2,2,32,2048]{4,3,0,1,2:T(8,128)(2,1)S(1)}, bf16[2,2,2,32,2048]{4,3,0,1,2:T(8,128)(2,1)S(1)}, u32[]{:S(2)}, u32[]{:S(2)}) %collective-permute-start.60) | collective-permute-done | bytes 1048608 | tf_op jit(solution)/shard_map/ppermute | solution.py:42
  676.6 18.4 %collective-permute-done.70 = bf16[2,2,2,64,1024]{4,3,0,1,2:T(8,128)(2,1)S(1)} collective-permute-done((bf16[2,2,2,64,1024]{4,3,0,1,2:T(8,128)(2,1)S(1)}, bf16[2,2,2,64,1024]{4,3,0,1,2:T(8,128)(2,1)S(1)}, u32[]{:S(2)}, u32[]{:S(2)}) %collective-permute-start.70) | collective-permute-done | bytes 1048608 | tf_op jit(solution)/shard_map/ppermute | solution.py:42
  697.1 17.4 %collective-permute-done.61 = bf16[2,2,32,2048]{3,2,0,1:T(8,128)(2,1)S(1)} collective-permute-done((bf16[2,2,32,2048]{3,2,0,1:T(8,128)(2,1)S(1)}, bf16[2,2,32,2048]{3,2,0,1:T(8,128)(2,1)S(1)}, u32[]{:S(2)}, u32[]{:S(2)}) %collective-permute-start.61) | collective-permute-done | bytes 524320 | tf_op jit(solution)/shard_map/ppermute | solution.py:42
  717.0 7.0 collective-permute-done.71
  734.1 8.0 collective-permute-done.63
  745.1 8.9 while.32
  755.9 5.5 multiply_reduce_fusion.5
  761.5 5.9 fusion.124
  788.1 14.5 %fusion.54 = f32[2,256,24,64]{1,3,2,0:T(8,128)} fusion(f32[2,256,24,64]{1,3,2,0:T(8,128)} %get-tuple-element.656, f32[2,256,24,64]{1,3,2,0:T(8,128)S(1)} %bitcast.737, f32[2,24,64,256]{3,2,1,0:T(8,128)S(1)} %bitcast.738, f32[2,256,24]{1,2,0:T(8,128)} %copy.643, f32[2,256,24]{1,2,0:T(8,128)} %copy.641, f32[2,256,256]{2,1,0:T(8,128)} %fusion.160, ...), kind=kOutput, calls=%fused_computation.113 | convolution fusion | flops 2434793472 | bytes 13385824 | tf_op jit(solution)/shard_map/transpose(jvp(vmap(ijh,jhp->ihp)))/dot_general | solution.py:223
  807.3 10.2 %multiply_reduce_fusion.3 = (f32[1792]{0:T(1024)S(1)}, f32[1792]{0:T(1024)}, f32[1792]{0:T(1024)}, f32[1792]{0:T(1024)S(1)}, bf16[1792]{0:T(1024)(128)(2,1)}, /*index=5*/f32[2,256,1792]{2,1,0:T(8,128)S(1)}) fusion(f32[2,256,1792]{2,1,0:T(8,128)} %bitcast.746, f32[2,3,1792]{2,1,0:T(4,128)} %collective-permute-done.6, pred[2,256]{1,0:T(4,128)(4,1)} %get-tuple-element.629, ...), kind=kLoop, calls=%fused_computation.100 | loop fusion | flops 24763648 | bytes 18427392 | tf_op jit(solution)/shard_map/transpose(jvp())/reduce_sum | solution.py:193
  832.0 6.1 fusion.70
  838.3 7.2 fusion.95
  887.7 20.4 %collective-permute-done.40 = bf16[2,2,2,32,2432]{4,3,0,1,2:T(8,128)(2,1)S(1)} collective-permute-done((bf16[2,2,2,32,2432]{4,3,0,1,2:T(8,128)(2,1)S(1)}, bf16[2,2,2,32,2432]{4,3,0,1,2:T(8,128)(2,1)S(1)}, u32[]{:S(2)}, u32[]{:S(2)}) %collective-permute-start.40) | collective-permute-done | bytes 1245216 | tf_op jit(solution)/shard_map/ppermute | solution.py:42
  909.0 5.6 collective-permute-done.45
  916.1 8.5 collective-permute-done.41
  925.9 8.4 collective-permute-done.42
  935.8 5.0 collective-permute-done.43
  947.2 5.9 collective-permute-done.48
  (863 shorter events, 481.4 us)
Async XLA Ops:
  7.2 386.2 %all-gather.5.cloned.1.call-start = ((), (), s32[]{:S(2)}) async-start(), calls=%async_computation | async-start | bytes 3932160 | tf_op jit(solution)/shard_map/all_gather | solution.py:96
  13.5 48.6 %collective-permute-start = (bf16[32,2432]{1,0:T(8,128)(2,1)}, bf16[32,2432]{1,0:T(8,128)(2,1)S(1)}, u32[]{:S(2)}, u32[]{:S(2)}) collective-permute-start(bf16[32,2432]{1,0:T(8,128)(2,1)} %pad_maximum_fusion.43), channel_id=1, source_target_pairs={{0,16},{4,20},{8,24},{12,28},{16,0},{20,4},{24,8},{28,12},{1,17},{... | collective-permute-start | bytes 466952 | tf_op jit(solution)/shard_map/ppermute | solution.py:42
  18.2 22.8 %collective-permute-start.19 = (bf16[2,256]{1,0:T(2,128)(2,1)S(1)}, bf16[2,256]{1,0:T(2,128)(2,1)S(1)}, u32[]{:S(2)}, u32[]{:S(2)}) collective-permute-start(bf16[2,256]{1,0:T(2,128)(2,1)S(1)} %get-tuple-element.641), channel_id=1, source_target_pairs={{0,2},{1,3},{2,0},{3,1},{4,6},{5,7},{6,4},{7,5},{8,10},{9,11},{10,... | collective-permute-start | bytes 3080 | tf_op jit(solution)/shard_map/ppermute | solution.py:42
  22.7 43.1 %collective-permute-start.7 = (bf16[32,2560]{1,0:T(8,128)(2,1)}, bf16[32,2560]{1,0:T(8,128)(2,1)}, u32[]{:S(2)}, u32[]{:S(2)}) collective-permute-start(bf16[32,2560]{1,0:T(8,128)(2,1)} %constant_dynamic-update-slice_fusion), channel_id=1, source_target_pairs={{0,16},{4,20},{8,24},{12,28},{16,0},{20,4},{24,8},{28,12},{1,17},{... | collective-permute-start | bytes 491528 | tf_op jit(solution)/shard_map/ppermute | solution.py:42
  26.0 40.9 %collective-permute-start.12 = (bf16[80,1024]{1,0:T(8,128)(2,1)}, bf16[80,1024]{1,0:T(8,128)(2,1)}, u32[]{:S(2)}, u32[]{:S(2)}) collective-permute-start(bf16[80,1024]{1,0:T(8,128)(2,1)} %constant_dynamic-update-slice_fusion.2), channel_id=1, source_target_pairs={{0,16},{4,20},{8,24},{12,28},{16,0},{20,4},{24,8},{28,12},{1,17},{... | collective-permute-start | bytes 491528 | tf_op jit(solution)/shard_map/ppermute | solution.py:42
  65.8 19.1 %collective-permute-start.1 = (bf16[2,32,2432]{2,1,0:T(8,128)(2,1)S(1)}, bf16[2,32,2432]{2,1,0:T(8,128)(2,1)S(1)}, u32[]{:S(2)}, u32[]{:S(2)}) collective-permute-start(bf16[2,32,2432]{2,1,0:T(8,128)(2,1)S(1)} %pad_maximum_fusion.38), channel_id=1, source_target_pairs={{0,8},{4,12},{8,0},{12,4},{16,24},{20,28},{24,16},{28,20},{1,9},{5... | collective-permute-start | bytes 933896 | tf_op jit(solution)/shard_map/ppermute | solution.py:42
  67.0 24.9 %collective-permute-start.8 = (bf16[2,32,2560]{2,1,0:T(8,128)(2,1)S(1)}, bf16[2,32,2560]{2,1,0:T(8,128)(2,1)S(1)}, u32[]{:S(2)}, u32[]{:S(2)}) collective-permute-start(bf16[2,32,2560]{2,1,0:T(8,128)(2,1)S(1)} %pad_maximum_fusion.36), channel_id=1, source_target_pairs={{0,8},{4,12},{8,0},{12,4},{16,24},{20,28},{24,16},{28,20},{1,9},{5... | collective-permute-start | bytes 983048 | tf_op jit(solution)/shard_map/ppermute | solution.py:42
  70.1 28.4 %collective-permute-start.13 = (bf16[2,80,1024]{2,1,0:T(8,128)(2,1)S(1)}, bf16[2,80,1024]{2,1,0:T(8,128)(2,1)S(1)}, u32[]{:S(2)}, u32[]{:S(2)}) collective-permute-start(bf16[2,80,1024]{2,1,0:T(8,128)(2,1)S(1)} %pad_maximum_fusion.37), channel_id=1, source_target_pairs={{0,8},{4,12},{8,0},{12,4},{16,24},{20,28},{24,16},{28,20},{1,9},{5... | collective-permute-start | bytes 983048 | tf_op jit(solution)/shard_map/ppermute | solution.py:42
  72.6 27.6 %collective-permute-start.28 = (bf16[2,2,32,2048]{3,2,1,0:T(8,128)(2,1)S(1)}, bf16[2,2,32,2048]{3,2,1,0:T(8,128)(2,1)S(1)}, u32[]{:S(2)}, u32[]{:S(2)}) collective-permute-start(bf16[2,2,32,2048]{3,2,1,0:T(8,128)(2,1)S(1)} %pad_maximum_fusion.34), channel_id=1, source_target_pairs={{0,2},{1,3},{2,0},{3,1},{4,6},{5,7},{6,4},{7,5},{8,10},{9,11},{10,... | collective-permute-start | bytes 1572872 | tf_op jit(solution)/shard_map/ppermute | solution.py:42
  78.2 22.2 %collective-permute-start.33 = (bf16[2,2,64,1024]{3,2,1,0:T(8,128)(2,1)S(1)}, bf16[2,2,64,1024]{3,2,1,0:T(8,128)(2,1)S(1)}, u32[]{:S(2)}, u32[]{:S(2)}) collective-permute-start(bf16[2,2,64,1024]{3,2,1,0:T(8,128)(2,1)S(1)} %pad_maximum_fusion.35), channel_id=1, source_target_pairs={{0,4},{4,0},{8,12},{12,8},{16,20},{20,16},{24,28},{28,24},{1,5},{5... | collective-permute-start | bytes 1572872 | tf_op jit(solution)/shard_map/ppermute | solution.py:42
  84.9 19.3 %collective-permute-start.23 = (bf16[2,2,32,2048]{3,2,0,1:T(8,128)(2,1)S(1)}, bf16[2,2,32,2048]{3,2,0,1:T(8,128)(2,1)S(1)}, u32[]{:S(2)}, u32[]{:S(2)}) collective-permute-start(bf16[2,2,32,2048]{3,2,0,1:T(8,128)(2,1)S(1)} %pad_maximum_fusion.33), channel_id=1, source_target_pairs={{0,4},{4,0},{8,12},{12,8},{16,20},{20,16},{24,28},{28,24},{1,5},{5... | collective-permute-start | bytes 1572872 | tf_op jit(solution)/shard_map/ppermute | solution.py:42
  98.5 19.7 %collective-permute-start.9 = (bf16[2,2,32,2560]{3,2,1,0:T(8,128)(2,1)S(1)}, bf16[2,2,32,2560]{3,2,1,0:T(8,128)(2,1)S(1)}, u32[]{:S(2)}, u32[]{:S(2)}) collective-permute-start(bf16[2,2,32,2560]{3,2,1,0:T(8,128)(2,1)S(1)} %pad_maximum_fusion.29), channel_id=1, source_target_pairs={{0,4},{4,0},{8,12},{12,8},{16,20},{20,16},{24,28},{28,24},{1,5},{5... | collective-permute-start | bytes 1966088 | tf_op jit(solution)/shard_map/ppermute | solution.py:42
  100.2 22.8 %collective-permute-start.14 = (bf16[2,2,80,1024]{3,2,1,0:T(8,128)(2,1)S(1)}, bf16[2,2,80,1024]{3,2,1,0:T(8,128)(2,1)S(1)}, u32[]{:S(2)}, u32[]{:S(2)}) collective-permute-start(bf16[2,2,80,1024]{3,2,1,0:T(8,128)(2,1)S(1)} %pad_maximum_fusion.30), channel_id=1, source_target_pairs={{0,2},{1,3},{2,0},{3,1},{4,6},{5,7},{6,4},{7,5},{8,10},{9,11},{10,... | collective-permute-start | bytes 1966088 | tf_op jit(solution)/shard_map/ppermute | solution.py:42
  100.5 40.3 %collective-permute-start.29 = (bf16[2,2,2,32,2048]{4,3,2,1,0:T(8,128)(2,1)S(1)}, bf16[2,2,2,32,2048]{4,3,2,1,0:T(8,128)(2,1)S(1)}, u32[]{:S(2)}, u32[]{:S(2)}) collective-permute-start(bf16[2,2,2,32,2048]{4,3,2,1,0:T(8,128)(2,1)S(1)} %pad_maximum_fusion.26), channel_id=1, source_target_pairs={{0,4},{4,0},{8,12},{12,8},{16,20},{20,16},{24,28},{28,24},{1,5},{5... | collective-permute-start | bytes 3145736 | tf_op jit(solution)/shard_map/ppermute | solution.py:42
  104.2 41.2 %collective-permute-start.34 = (bf16[2,2,2,64,1024]{4,3,2,1,0:T(8,128)(2,1)S(1)}, bf16[2,2,2,64,1024]{4,3,2,1,0:T(8,128)(2,1)S(1)}, u32[]{:S(2)}, u32[]{:S(2)}) collective-permute-start(bf16[2,2,2,64,1024]{4,3,2,1,0:T(8,128)(2,1)S(1)} %pad_maximum_fusion.27), channel_id=1, source_target_pairs={{0,2},{1,3},{2,0},{3,1},{4,6},{5,7},{6,4},{7,5},{8,10},{9,11},{10,... | collective-permute-start | bytes 3145736 | tf_op jit(solution)/shard_map/ppermute | solution.py:42
  108.9 59.0 %collective-permute-start.24 = (bf16[2,2,2,32,2048]{4,3,0,1,2:T(8,128)(2,1)S(1)}, bf16[2,2,2,32,2048]{4,3,0,1,2:T(8,128)(2,1)S(1)}, u32[]{:S(2)}, u32[]{:S(2)}) collective-permute-start(bf16[2,2,2,32,2048]{4,3,0,1,2:T(8,128)(2,1)S(1)} %pad_maximum_fusion.25), channel_id=1, source_target_pairs={{0,2},{1,3},{2,0},{3,1},{4,6},{5,7},{6,4},{7,5},{8,10},{9,11},{10,... | collective-permute-start | bytes 3145736 | tf_op jit(solution)/shard_map/ppermute | solution.py:42
  118.3 50.2 %collective-permute-start.3 = (bf16[2,2,2,32,2432]{4,3,2,1,0:T(8,128)(2,1)S(1)}, bf16[2,2,2,32,2432]{4,3,2,1,0:T(8,128)(2,1)S(1)}, u32[]{:S(2)}, u32[]{:S(2)}) collective-permute-start(bf16[2,2,2,32,2432]{4,3,2,1,0:T(8,128)(2,1)S(1)} %pad_maximum_fusion.22), channel_id=1, source_target_pairs={{0,4},{4,0},{8,12},{12,8},{16,20},{20,16},{24,28},{28,24},{1,5},{5... | collective-permute-start | bytes 3735560 | tf_op jit(solution)/shard_map/ppermute | solution.py:42
  122.9 71.2 %collective-permute-start.10 = (bf16[2,2,2,32,2560]{4,3,2,1,0:T(8,128)(2,1)S(1)}, bf16[2,2,2,32,2560]{4,3,2,1,0:T(8,128)(2,1)S(1)}, u32[]{:S(2)}, u32[]{:S(2)}) collective-permute-start(bf16[2,2,2,32,2560]{4,3,2,1,0:T(8,128)(2,1)S(1)} %pad_maximum_fusion.20), channel_id=1, source_target_pairs={{0,2},{1,3},{2,0},{3,1},{4,6},{5,7},{6,4},{7,5},{8,10},{9,11},{10,... | collective-permute-start | bytes 3932168 | tf_op jit(solution)/shard_map/ppermute | solution.py:42
  140.7 55.6 %collective-permute-start.15 = (bf16[2,2,2,80,1024]{4,3,2,1,0:T(8,128)(2,1)S(1)}, bf16[2,2,2,80,1024]{4,3,2,1,0:T(8,128)(2,1)S(1)}, u32[]{:S(2)}, u32[]{:S(2)}) collective-permute-start(bf16[2,2,2,80,1024]{4,3,2,1,0:T(8,128)(2,1)S(1)} %pad_maximum_fusion.21), channel_id=1, source_target_pairs={{0,4},{4,0},{8,12},{12,8},{16,20},{20,16},{24,28},{28,24},{1,5},{5... | collective-permute-start | bytes 3932168 | tf_op jit(solution)/shard_map/ppermute | solution.py:42
  145.4 54.5 %collective-permute-start.30 = (bf16[2,2,2,2,32,2048]{5,4,3,2,1,0:T(8,128)(2,1)S(1)}, bf16[2,2,2,2,32,2048]{5,4,3,2,1,0:T(8,128)(2,1)S(1)}, u32[]{:S(2)}, u32[]{:S(2)}) collective-permute-start(bf16[2,2,2,2,32,2048]{5,4,3,2,1,0:T(8,128)(2,1)S(1)} %pad_maximum_fusion.13), channel_id=1, source_target_pairs={{0,1},{1,0},{2,3},{3,2},{4,5},{5,4},{6,7},{7,6},{8,9},{9,8},{10,11... | collective-permute-start | bytes 6291464 | tf_op jit(solution)/shard_map/ppermute | solution.py:42
  167.9 35.1 %collective-permute-start.35 = (bf16[2,2,2,2,64,1024]{5,4,3,2,1,0:T(8,128)(2,1)S(1)}, bf16[2,2,2,2,64,1024]{5,4,3,2,1,0:T(8,128)(2,1)S(1)}, u32[]{:S(2)}, u32[]{:S(2)}) collective-permute-start(bf16[2,2,2,2,64,1024]{5,4,3,2,1,0:T(8,128)(2,1)S(1)} %pad_maximum_fusion.14), channel_id=1, source_target_pairs={{0,1},{1,0},{2,3},{3,2},{4,5},{5,4},{6,7},{7,6},{8,9},{9,8},{10,11... | collective-permute-start | bytes 6291464 | tf_op jit(solution)/shard_map/ppermute | solution.py:42
  168.5 35.2 %collective-permute-start.25 = (bf16[2,2,2,2,32,2048]{5,4,3,2,1,0:T(8,128)(2,1)S(1)}, bf16[2,2,2,2,32,2048]{5,4,3,2,1,0:T(8,128)(2,1)}, u32[]{:S(2)}, u32[]{:S(2)}) collective-permute-start(bf16[2,2,2,2,32,2048]{5,4,3,2,1,0:T(8,128)(2,1)S(1)} %copy.762), channel_id=1, source_target_pairs={{0,1},{1,0},{2,3},{3,2},{4,5},{5,4},{6,7},{7,6},{8,9},{9,8},{10,11... | collective-permute-start | bytes 6291464 | tf_op jit(solution)/shard_map/ppermute | solution.py:42
  194.2 21.0 %collective-permute-start.4 = (bf16[2,2,2,2,32,2432]{5,4,3,2,1,0:T(8,128)(2,1)S(1)}, bf16[2,2,2,2,32,2432]{5,4,3,2,1,0:T(8,128)(2,1)S(1)}, u32[]{:S(2)}, u32[]{:S(2)}) collective-permute-start(bf16[2,2,2,2,32,2432]{5,4,3,2,1,0:T(8,128)(2,1)S(1)} %pad_maximum_fusion.10), channel_id=1, source_target_pairs={{0,1},{1,0},{2,3},{3,2},{4,5},{5,4},{6,7},{7,6},{8,9},{9,8},{10,11... | collective-permute-start | bytes 7471112 | tf_op jit(solution)/shard_map/ppermute | solution.py:42
  196.3 123.4 %collective-permute-start.11 = (bf16[2,2,2,2,32,2560]{5,4,3,2,1,0:T(8,128)(2,1)}, bf16[2,2,2,2,32,2560]{5,4,3,2,1,0:T(8,128)(2,1)}, u32[]{:S(2)}, u32[]{:S(2)}) collective-permute-start(bf16[2,2,2,2,32,2560]{5,4,3,2,1,0:T(8,128)(2,1)} %pad_maximum_fusion.7), channel_id=1, source_target_pairs={{0,1},{1,0},{2,3},{3,2},{4,5},{5,4},{6,7},{7,6},{8,9},{9,8},{10,11... | collective-permute-start | bytes 7864328 | tf_op jit(solution)/shard_map/ppermute | solution.py:42
  199.9 130.3 %collective-permute-start.16 = (bf16[2,2,2,2,80,1024]{5,4,3,2,1,0:T(8,128)(2,1)}, bf16[2,2,2,2,80,1024]{5,4,3,2,1,0:T(8,128)(2,1)}, u32[]{:S(2)}, u32[]{:S(2)}) collective-permute-start(bf16[2,2,2,2,80,1024]{5,4,3,2,1,0:T(8,128)(2,1)} %pad_maximum_fusion.8), channel_id=1, source_target_pairs={{0,1},{1,0},{2,3},{3,2},{4,5},{5,4},{6,7},{7,6},{8,9},{9,8},{10,11... | collective-permute-start | bytes 7864328 | tf_op jit(solution)/shard_map/ppermute | solution.py:42
  246.5 80.3 %collective-permute-start.17 = (bf16[2,256,4,128]{3,1,2,0:T(8,128)(2,1)}, bf16[2,256,4,128]{3,1,2,0:T(8,128)(2,1)}, u32[]{:S(2)}, u32[]{:S(2)}) collective-permute-start(bf16[2,256,4,128]{3,1,2,0:T(8,128)(2,1)} %pad_maximum_fusion.32), channel_id=1, source_target_pairs={{0,2},{1,3},{2,0},{3,1},{4,6},{5,7},{6,4},{7,5},{8,10},{9,11},{10,... | collective-permute-start | bytes 1572872 | tf_op jit(solution)/shard_map/ppermute | solution.py:42
  249.8 42.1 %collective-permute-start.6 = (f32[2,3,1792]{2,1,0:T(4,128)}, f32[2,3,1792]{2,1,0:T(4,128)}, u32[]{:S(2)}, u32[]{:S(2)}) collective-permute-start(f32[2,3,1792]{2,1,0:T(4,128)} %slice.337), channel_id=1, source_target_pairs={{0,1},{1,2},{2,3},{4,5},{5,6},{6,7},{8,9},{9,10},{10,11},{12,13},{... | collective-permute-start | bytes 129032 | tf_op jit(solution)/shard_map/ppermute | solution.py:24
  317.0 428.1 %all-gather.7.cloned.1.call-start = ((), (), s32[]{:S(2)}) async-start(), calls=%async_computation.1 | async-start | bytes 3932160 | tf_op jit(solution)/shard_map/all_gather | solution.py:119
  329.7 24.3 %collective-permute-start.18 = (bf16[2,2,256,4,128]{4,2,3,1,0:T(8,128)(2,1)}, bf16[2,2,256,4,128]{4,2,3,1,0:T(8,128)(2,1)}, u32[]{:S(2)}, u32[]{:S(2)}) collective-permute-start(bf16[2,2,256,4,128]{4,2,3,1,0:T(8,128)(2,1)} %pad_maximum_fusion.23), channel_id=1, source_target_pairs={{0,1},{1,0},{2,3},{3,2},{4,5},{5,4},{6,7},{7,6},{8,9},{9,8},{10,11... | collective-permute-start | bytes 3145736 | tf_op jit(solution)/shard_map/ppermute | solution.py:42
  597.5 29.6 %collective-permute-start.37 = (bf16[2,2,256,4,128]{4,2,3,1,0:T(8,128)(2,1)}, bf16[2,2,256,4,128]{4,2,3,1,0:T(8,128)(2,1)}, u32[]{:S(2)}, u32[]{:S(2)}) collective-permute-start(bf16[2,2,256,4,128]{4,2,3,1,0:T(8,128)(2,1)} %dynamic-slice_bitcast_fusion.6), channel_id=1, source_target_pairs={{0,1},{1,0},{2,3},{3,2},{4,5},{5,4},{6,7},{7,6},{8,9},{9,8},{10,11... | collective-permute-start | bytes 3145736 | tf_op jit(solution)/shard_map/ppermute | solution.py:42
  612.9 39.4 %collective-permute-start.54 = (bf16[2,2,2,2,80,1024]{5,4,0,1,3,2:T(8,128)(2,1)S(1)}, bf16[2,2,2,2,80,1024]{5,4,0,1,3,2:T(8,128)(2,1)S(1)}, u32[]{:S(2)}, u32[]{:S(2)}) collective-permute-start(bf16[2,2,2,2,80,1024]{5,4,0,1,3,2:T(8,128)(2,1)S(1)} %bitcast.797), channel_id=1, source_target_pairs={{0,1},{1,0},{2,3},{3,2},{4,5},{5,4},{6,7},{7,6},{8,9},{9,8},{10,11... | collective-permute-start | bytes 7864328 | tf_op jit(solution)/shard_map/ppermute | solution.py:42
  615.6 29.8 %collective-permute-start.59 = (bf16[2,2,2,2,32,2048]{5,4,0,1,2,3:T(8,128)(2,1)S(1)}, bf16[2,2,2,2,32,2048]{5,4,0,1,2,3:T(8,128)(2,1)S(1)}, u32[]{:S(2)}, u32[]{:S(2)}) collective-permute-start(bf16[2,2,2,2,32,2048]{5,4,0,1,2,3:T(8,128)(2,1)S(1)} %bitcast.806), channel_id=1, source_target_pairs={{0,1},{1,0},{2,3},{3,2},{4,5},{5,4},{6,7},{7,6},{8,9},{9,8},{10,11... | collective-permute-start | bytes 6291464 | tf_op jit(solution)/shard_map/ppermute | solution.py:42
  618.4 29.6 %collective-permute-start.64 = (bf16[2,2,2,2,32,2048]{5,4,0,1,3,2:T(8,128)(2,1)S(1)}, bf16[2,2,2,2,32,2048]{5,4,0,1,3,2:T(8,128)(2,1)S(1)}, u32[]{:S(2)}, u32[]{:S(2)}) collective-permute-start(bf16[2,2,2,2,32,2048]{5,4,0,1,3,2:T(8,128)(2,1)S(1)} %bitcast.805), channel_id=1, source_target_pairs={{0,1},{1,0},{2,3},{3,2},{4,5},{5,4},{6,7},{7,6},{8,9},{9,8},{10,11... | collective-permute-start | bytes 6291464 | tf_op jit(solution)/shard_map/ppermute | solution.py:42
  623.4 27.1 %collective-permute-start.69 = (bf16[2,2,2,2,64,1024]{5,4,0,1,2,3:T(8,128)(2,1)S(1)}, bf16[2,2,2,2,64,1024]{5,4,0,1,2,3:T(8,128)(2,1)S(1)}, u32[]{:S(2)}, u32[]{:S(2)}) collective-permute-start(bf16[2,2,2,2,64,1024]{5,4,0,1,2,3:T(8,128)(2,1)S(1)} %bitcast.804), channel_id=1, source_target_pairs={{0,1},{1,0},{2,3},{3,2},{4,5},{5,4},{6,7},{7,6},{8,9},{9,8},{10,11... | collective-permute-start | bytes 6291464 | tf_op jit(solution)/shard_map/ppermute | solution.py:42
  646.4 26.2 %collective-permute-start.60 = (bf16[2,2,2,32,2048]{4,3,0,1,2:T(8,128)(2,1)S(1)}, bf16[2,2,2,32,2048]{4,3,0,1,2:T(8,128)(2,1)S(1)}, u32[]{:S(2)}, u32[]{:S(2)}) collective-permute-start(bf16[2,2,2,32,2048]{4,3,0,1,2:T(8,128)(2,1)S(1)} %dynamic-slice_bitcast_fusion.5), channel_id=1, source_target_pairs={{0,2},{1,3},{2,0},{3,1},{4,6},{5,7},{6,4},{7,5},{8,10},{9,11},{10,... | collective-permute-start | bytes 3145736 | tf_op jit(solution)/shard_map/ppermute | solution.py:42
  649.0 26.2 %collective-permute-start.65 = (bf16[2,2,2,32,2048]{4,3,0,1,2:T(8,128)(2,1)S(1)}, bf16[2,2,2,32,2048]{4,3,0,1,2:T(8,128)(2,1)S(1)}, u32[]{:S(2)}, u32[]{:S(2)}) collective-permute-start(bf16[2,2,2,32,2048]{4,3,0,1,2:T(8,128)(2,1)S(1)} %dynamic-slice_bitcast_fusion.4), channel_id=1, source_target_pairs={{0,4},{4,0},{8,12},{12,8},{16,20},{20,16},{24,28},{28,24},{1,5},{5... | collective-permute-start | bytes 3145736 | tf_op jit(solution)/shard_map/ppermute | solution.py:42
  651.6 43.4 %collective-permute-start.70 = (bf16[2,2,2,64,1024]{4,3,0,1,2:T(8,128)(2,1)S(1)}, bf16[2,2,2,64,1024]{4,3,0,1,2:T(8,128)(2,1)S(1)}, u32[]{:S(2)}, u32[]{:S(2)}) collective-permute-start(bf16[2,2,2,64,1024]{4,3,0,1,2:T(8,128)(2,1)S(1)} %dynamic-slice_bitcast_fusion.3), channel_id=1, source_target_pairs={{0,2},{1,3},{2,0},{3,1},{4,6},{5,7},{6,4},{7,5},{8,10},{9,11},{10,... | collective-permute-start | bytes 3145736 | tf_op jit(solution)/shard_map/ppermute | solution.py:42
  653.9 70.4 %collective-permute-start.55 = (bf16[2,2,2,80,1024]{4,3,0,1,2:T(8,128)(2,1)S(1)}, bf16[2,2,2,80,1024]{4,3,0,1,2:T(8,128)(2,1)S(1)}, u32[]{:S(2)}, u32[]{:S(2)}) collective-permute-start(bf16[2,2,2,80,1024]{4,3,0,1,2:T(8,128)(2,1)S(1)} %dynamic-slice_bitcast_fusion), channel_id=1, source_target_pairs={{0,4},{4,0},{8,12},{12,8},{16,20},{20,16},{24,28},{28,24},{1,5},{5... | collective-permute-start | bytes 3932168 | tf_op jit(solution)/shard_map/ppermute | solution.py:42
  673.0 41.5 %collective-permute-start.61 = (bf16[2,2,32,2048]{3,2,0,1:T(8,128)(2,1)S(1)}, bf16[2,2,32,2048]{3,2,0,1:T(8,128)(2,1)S(1)}, u32[]{:S(2)}, u32[]{:S(2)}) collective-permute-start(bf16[2,2,32,2048]{3,2,0,1:T(8,128)(2,1)S(1)} %dynamic-slice_bitcast_fusion.12), channel_id=1, source_target_pairs={{0,4},{4,0},{8,12},{12,8},{16,20},{20,16},{24,28},{28,24},{1,5},{5... | collective-permute-start | bytes 1572872 | tf_op jit(solution)/shard_map/ppermute | solution.py:42
  675.6 39.1 %collective-permute-start.66 = (bf16[2,2,32,2048]{3,2,0,1:T(8,128)(2,1)S(1)}, bf16[2,2,32,2048]{3,2,0,1:T(8,128)(2,1)S(1)}, u32[]{:S(2)}, u32[]{:S(2)}) collective-permute-start(bf16[2,2,32,2048]{3,2,0,1:T(8,128)(2,1)S(1)} %dynamic-slice_bitcast_fusion.11), channel_id=1, source_target_pairs={{0,2},{1,3},{2,0},{3,1},{4,6},{5,7},{6,4},{7,5},{8,10},{9,11},{10,... | collective-permute-start | bytes 1572872 | tf_op jit(solution)/shard_map/ppermute | solution.py:42
  695.5 28.4 %collective-permute-start.71 = (bf16[2,2,64,1024]{3,2,0,1:T(8,128)(2,1)S(1)}, bf16[2,2,64,1024]{3,2,0,1:T(8,128)(2,1)S(1)}, u32[]{:S(2)}, u32[]{:S(2)}) collective-permute-start(bf16[2,2,64,1024]{3,2,0,1:T(8,128)(2,1)S(1)} %dynamic-slice_bitcast_fusion.10), channel_id=1, source_target_pairs={{0,4},{4,0},{8,12},{12,8},{16,20},{20,16},{24,28},{28,24},{1,5},{5... | collective-permute-start | bytes 1572872 | tf_op jit(solution)/shard_map/ppermute | solution.py:42
  726.8 138.9 %collective-permute-start.56 = (bf16[2,2,80,1024]{3,2,0,1:T(8,128)(2,1)}, bf16[2,2,80,1024]{3,2,0,1:T(8,128)(2,1)}, u32[]{:S(2)}, u32[]{:S(2)}) collective-permute-start(bf16[2,2,80,1024]{3,2,0,1:T(8,128)(2,1)} %dynamic-slice_bitcast_fusion.7), channel_id=1, source_target_pairs={{0,2},{1,3},{2,0},{3,1},{4,6},{5,7},{6,4},{7,5},{8,10},{9,11},{10,... | collective-permute-start | bytes 1966088 | tf_op jit(solution)/shard_map/ppermute | solution.py:42
  734.1 137.5 %collective-permute-start.73 = (bf16[64,1024]{1,0:T(8,128)(2,1)}, bf16[64,1024]{1,0:T(8,128)(2,1)}, u32[]{:S(2)}, u32[]{:S(2)}) collective-permute-start(bf16[64,1024]{1,0:T(8,128)(2,1)} %dynamic-slice_bitcast_fusion.23), channel_id=1, source_target_pairs={{0,16},{4,20},{8,24},{12,28},{16,0},{20,4},{24,8},{28,12},{1,17},{... | collective-permute-start | bytes 393224 | tf_op jit(solution)/shard_map/ppermute | solution.py:42
  828.0 28.5 %collective-permute-start.49 = (f32[3,24]{1,0:T(4,128)}, f32[3,24]{1,0:T(4,128)}, u32[]{:S(2)}, u32[]{:S(2)}) collective-permute-start(f32[3,24]{1,0:T(4,128)} %pad_maximum_fusion.49), channel_id=1, source_target_pairs={{0,1},{1,0},{2,3},{3,2},{4,5},{5,4},{6,7},{7,6},{8,9},{9,8},{10,11... | collective-permute-start | bytes 872 | tf_op jit(solution)/shard_map/ppermute | solution.py:42
  856.4 23.9 %collective-permute-start.39 = (bf16[2,2,2,2,32,2432]{5,4,0,1,3,2:T(8,128)(2,1)S(1)}, bf16[2,2,2,2,32,2432]{5,4,0,1,3,2:T(8,128)(2,1)S(1)}, u32[]{:S(2)}, u32[]{:S(2)}) collective-permute-start(bf16[2,2,2,2,32,2432]{5,4,0,1,3,2:T(8,128)(2,1)S(1)} %bitcast.799), channel_id=1, source_target_pairs={{0,1},{1,0},{2,3},{3,2},{4,5},{5,4},{6,7},{7,6},{8,9},{9,8},{10,11... | collective-permute-start | bytes 7471112 | tf_op jit(solution)/shard_map/ppermute | solution.py:42
  863.3 19.2 %collective-permute-start.44 = (bf16[2,2,2,2,32,2560]{5,4,0,1,2,3:T(8,128)(2,1)S(1)}, bf16[2,2,2,2,32,2560]{5,4,0,1,2,3:T(8,128)(2,1)S(1)}, u32[]{:S(2)}, u32[]{:S(2)}) collective-permute-start(bf16[2,2,2,2,32,2560]{5,4,0,1,2,3:T(8,128)(2,1)S(1)} %bitcast.798), channel_id=1, source_target_pairs={{0,1},{1,0},{2,3},{3,2},{4,5},{5,4},{6,7},{7,6},{8,9},{9,8},{10,11... | collective-permute-start | bytes 7864328 | tf_op jit(solution)/shard_map/ppermute | solution.py:42
  881.1 27.0 %collective-permute-start.40 = (bf16[2,2,2,32,2432]{4,3,0,1,2:T(8,128)(2,1)S(1)}, bf16[2,2,2,32,2432]{4,3,0,1,2:T(8,128)(2,1)S(1)}, u32[]{:S(2)}, u32[]{:S(2)}) collective-permute-start(bf16[2,2,2,32,2432]{4,3,0,1,2:T(8,128)(2,1)S(1)} %dynamic-slice_bitcast_fusion.2), channel_id=1, source_target_pairs={{0,4},{4,0},{8,12},{12,8},{16,20},{20,16},{24,28},{28,24},{1,5},{5... | collective-permute-start | bytes 3735560 | tf_op jit(solution)/shard_map/ppermute | solution.py:42
  883.4 31.3 %collective-permute-start.45 = (bf16[2,2,2,32,2560]{4,3,0,1,2:T(8,128)(2,1)S(1)}, bf16[2,2,2,32,2560]{4,3,0,1,2:T(8,128)(2,1)S(1)}, u32[]{:S(2)}, u32[]{:S(2)}) collective-permute-start(bf16[2,2,2,32,2560]{4,3,0,1,2:T(8,128)(2,1)S(1)} %dynamic-slice_bitcast_fusion.1), channel_id=1, source_target_pairs={{0,2},{1,3},{2,0},{3,1},{4,6},{5,7},{6,4},{7,5},{8,10},{9,11},{10,... | collective-permute-start | bytes 3932168 | tf_op jit(solution)/shard_map/ppermute | solution.py:42
  (194 other events, 2135.1 us)
Sparse Core Ops, SparseCore 0:
  317.2 27.7 all-gather.4
  561.4 27.6 all-gather.6

commit v2 on v1

--- a/solution.py
+++ b/solution.py
@@ -13,7 +13,7 @@
 
 
 epsilon = 1e-05
-highest = lax.Precision.HIGHEST
+highest = lax.Precision.HIGH
 rope_base = 100000000000.0
 masked_score = -1e30
 
@@ -62,10 +62,10 @@
     return block.reshape((-1,) + block.shape[len(seen) :])
 
 
-def shrunk(blocks, order):
+def shrunk(blocks, order, gates=()):
     left = list(order)
     total = blocks.reshape((2,) * len(left) + blocks.shape[1:])
-    for bit in order:
+    for stage, bit in enumerate(order):
         place = sum(bit_weight(b) > bit_weight(bit) for b in left)
         here = bit_value(bit)
         away = lax.dynamic_index_in_dim(total, 1 - here, place, keepdims=False)
@@ -73,6 +73,8 @@
         added = keep.astype(jnp.float32) + exchanged(away, bit).astype(jnp.float32)
         left.remove(bit)
         total = added.astype(jnp.bfloat16) if left else added
+        if stage < len(gates) and gates[stage] is not None:
+            total, _ = lax.optimization_barrier((total, gates[stage]))
     return total
 
 
@@ -80,8 +82,8 @@
     return grown(shard, halving_order(first_dp))
 
 
-def scatter_rows(partial, rows, first_dp):
-    return shrunk(partial.reshape((-1, rows) + partial.shape[1:]), halving_order(first_dp))
+def scatter_rows(partial, rows, first_dp, gates=()):
+    return shrunk(partial.reshape((-1, rows) + partial.shape[1:]), halving_order(first_dp), gates)
 
 
 def butterfly_sum(value):
@@ -303,6 +305,11 @@
     pack_one = gather_rows(jnp.concatenate([gate_proj, query_proj], axis=1), False).reshape(
         -1, 2560
     )
+    mamba_proj, attn_proj, feed_gate, feed_up, feed_down, pack_one, pack_two = (
+        lax.optimization_barrier(
+            (mamba_proj, attn_proj, feed_gate, feed_up, feed_down, pack_one, pack_two)
+        )
+    )
     pack_mix = gather_rows(jnp.concatenate([mamba_proj, attn_proj], axis=0), True)
     mamba_whole = pack_mix[:, :inner_rows].reshape(-1, pack_mix.shape[-1])
     attn_whole = pack_mix[:, inner_rows:].reshape(-1, pack_mix.shape[-1])
@@ -543,9 +550,10 @@
         jnp.concatenate([grad_step, small_grads], axis=1), ((0, 0), (0, 128 - MH - 16))
     )
     low = jnp.bfloat16
-    own_down = scatter_rows(grad_feed_down.astype(low), down_rows, False)
-    own_gate = scatter_rows(grad_feed_gate.astype(low), shard_rows, False)
-    own_up = scatter_rows(grad_feed_up.astype(low), shard_rows, True)
+    gates = (grad_queries, front_grads[5], summary_grads[2])
+    own_down = scatter_rows(grad_feed_down.astype(low), down_rows, False, gates)
+    own_gate = scatter_rows(grad_feed_gate.astype(low), shard_rows, False, gates)
+    own_up = scatter_rows(grad_feed_up.astype(low), shard_rows, True, gates)
     own_mix = scatter_rows(
         jnp.concatenate(
             [
@@ -556,6 +564,7 @@
         ).reshape(device_count * (inner_rows + attn_rows), -1),
         inner_rows + attn_rows,
         True,
+        gates,
     )
     own_one = scatter_rows(grad_one.astype(low), shard_rows, False)
     own_two = scatter_rows(

time: 968 us -> 953 us (0.985)
  waiting for transfers between devices: 269 us -> 235 us
  matrix products: 236 us -> 204 us
  other arithmetic: 191 us -> 208 us
  starting transfers between devices: 65 us -> 82 us
  local copies, waits for them, and re-layouts: 177 us -> 187 us
    ppermute x71, waiting for transfers between devices: 269 us -> 235 us  [exchanged(): return lax.ppermute(block, bit[0], route)]
    dot_general x3, matrix products: 55.6 us -> 37.3 us  [block_output(): result = jnp.einsum('ijh,jhp->ihp', kernel, inner_vals, precision=highest)]
    another operation x66 -> x67, other arithmetic: 32.3 us -> 49.6 us  [grown(): jnp.stack([jnp.where(low_half, block, other), jnp.where(low_half, other,...]
    convert_element_type x25, other arithmetic: 12.2 us -> 24.6 us  [shrunk(): total = added.astype(jnp.bfloat16) if left else added]
    unnamed x349 -> x415, local copies, waits for them, and re-layouts: 37.7 us -> 39.4 us
  transfers between devices with their start and end apart: 76 -> 76, of which waited for: 37 -> 28; matrix products, arithmetic and copies ran while one was open for 43% -> 43% of each run, Pallas kernels for 0% -> 0%
where the time goes in v2:
time: 953 us; the launch traced here: 940 us
  waiting for transfers between devices  235 us (25%)
  other arithmetic  208 us (22%)
  matrix products  204 us (21%)
  local copies, waits for them, and re-layouts  187 us (20%)
  starting transfers between devices  82 us (9%)
  between operations  18 us (2%)
    ppermute x71, waiting for transfers between devices, exchanged(): return lax.ppermute(block, bit[0], route)  235 us
    ppermute x71, starting transfers between devices, exchanged(): return lax.ppermute(block, bit[0], route)  66.6 us
    another operation x67, other arithmetic, grown(): jnp.stack([jnp.where(low_half, block, other), jnp.where(low_half, other,...  49.6 us
    unnamed x415, local copies, waits for them, and re-layouts  39.4 us
    dot_general x3, matrix products, block_output(): result = jnp.einsum('ijh,jhp->ihp', kernel, inner_vals, precision=highest)  37.3 us
    dot_general x7, matrix products, back_mul(): lax.dot_general(grad_rows, weight, (((1,), (1,)), ((), ())), preferred_el...  30.9 us
    dot_general x8, matrix products, outer_sum(): lax.dot_general(left, right, (((0,), (0,)), ((), ())), preferred_element_...  30.9 us
    dot_general x7, matrix products, forward_mul(): return jnp.dot(left, right, preferred_element_type=jnp.float32)  29.4 us
  transfers between devices with their start and end apart: 76, of which 28 were waited for; matrix products, arithmetic and copies ran while one was open for 43% of the time, Pallas kernels for 0%

profile of v2, /device:TPU:0, one launch (start us, length us, event | category | flops | bytes accessed | tf_op | source)
XLA Modules:
  0.0 940.2 jit_solution(16300806040417194126)
XLA Ops:
  36.5 7.9 collective-permute-done.6
  44.7 4.7 collective-permute-done.1
  51.1 7.8 collective-permute-done.7
  60.7 6.5 collective-permute-done.2
  68.8 22.1 %collective-permute-done.8 = bf16[2,2,2,32,2432]{4,3,2,1,0:T(8,128)(2,1)S(1)} collective-permute-done((bf16[2,2,2,32,2432]{4,3,2,1,0:T(8,128)(2,1)S(1)}, bf16[2,2,2,32,2432]{4,3,2,1,0:T(8,128)(2,1)S(1)}, u32[]{:S(2)}, u32[]{:S(2)}) %collective-permute-start.8) | collective-permute-done | bytes 1245216 | tf_op jit(solution)/shard_map/ppermute | solution.py:42
  119.8 5.3 fusion.216
  134.7 5.1 fusion.217
  184.6 5.6 reshape.930
  190.1 6.2 copy.656
  196.4 5.5 all_gather.18
  203.3 11.5 %fusion.50 = (f32[2,256,1792]{2,1,0:T(8,128)S(1)}, f32[2,256,1792]{2,1,0:T(8,128)}) fusion(f32[2,256,1792]{2,1,0:T(8,128)} %bitcast.741, pred[2,256]{1,0:T(4,128)(4,1)S(1)} %copy-done.165, f32[1792]{0:T(1024)S(1)} %mul.799, f32[2,3,1792]{2,1,0:T(4,128)} %collective-permute-done.11, pred[2,256]{1,0:T(4,128)(4,1)S(1)} %copy-done.169, f32[1792]{0:T(1024)S(1)} %mul.796, ...), kind=kLoop, calls=%fused_computation.107 | loop fusion | flops 17432576 | bytes 11090944 | tf_op jit(solution)/shard_map/jvp(jit(silu))/mul | solution.py:200
  226.5 9.8 %all-gather.7.cloned.1.call-start = ((), (), s32[]{:S(2)}) async-start(), calls=%async_computation.1 | async-start | bytes 3932160 | tf_op jit(solution)/shard_map/all_gather | solution.py:121
  255.2 4.7 collective-permute-done.32
  261.5 4.5 collective-permute-done.13
  275.7 8.2 collective-permute-done.14
  290.1 7.5 fusion.15
  297.6 9.2 exponential_reduce_fusion
  314.1 12.9 %collective-permute-done.34 = bf16[2,2,2,64,1024]{4,3,2,1,0:T(8,128)(2,1)} collective-permute-done((bf16[2,2,2,64,1024]{4,3,2,1,0:T(8,128)(2,1)}, bf16[2,2,2,64,1024]{4,3,2,1,0:T(8,128)(2,1)}, u32[]{:S(2)}, u32[]{:S(2)}) %collective-permute-start.34) | collective-permute-done | bytes 1048608 | tf_op jit(solution)/shard_map/ppermute | solution.py:42
  331.0 6.1 fusion.116
  365.7 6.3 while.31
  375.0 12.1 %multiply_reduce_fusion.10 = (f32[2,256]{1,0:T(2,128)S(1)}, f32[2,256,24,64]{1,3,2,0:T(8,128)}) fusion(f32[2,256,24,64]{1,3,2,0:T(8,128)} %copy.656, f32[2,256,24,64]{1,3,2,0:T(8,128)S(1)} %bitcast.737, f32[24]{0:T(128)S(1)} %copy-done.188, f32[2,256,24,64]{1,3,2,0:T(8,128)S(1)} %fusion.157, f32[2,256,24]{1,2,0:T(8,128)S(1)} %copy-done.120, ...), kind=kOutput, calls=%fused_computation.126 | convolution fusion | flops 1232338432 | bytes 13387872 | tf_op jit(solution)/shard_map/jvp(vmap(ijh,jhp->ihp))/dot_general | solution.py:225
  387.1 6.1 copy.759
  396.7 6.6 reshape.929
  419.4 8.0 fusion.37
  448.5 4.7 convolution_convert_fusion.3
  477.4 11.7 %fusion.118 = bf16[2,1024,2,128]{1,3,2,0:T(8,128)(2,1)} fusion(bf16[2,256,2,4,128]{1,4,3,2,0:T(8,128)(2,1)} %copy.696, f32[2,2,1024,256,4]{3,2,4,1,0:T(8,128)} %get-tuple-element.686, f32[2,2,4,256]{3,2,1,0:T(4,128)S(1)} %bitcast.815, pred[2,256,1024]{1,2,0:T(8,128)(4,1)S(1)} %compare_and_fusion), kind=kOutput, calls=%fused_computation.245 | convolution fusion | flops 1091043328 | bytes 19415040 | tf_op jit(solution)/shard_map/skgij,sikgd->sjkd/dot_general | solution.py:469
  489.1 13.4 %fusion.2 = (f32[2,2,4,256]{3,2,1,0:T(4,128)S(1)}, f32[2,2,1024,256,4]{3,2,4,1,0:T(8,128)}) fusion(f32[2,2,1024,256,4]{3,2,4,1,0:T(8,128)} %get-tuple-element.686, f32[2,2,4,256]{3,2,1,0:T(4,128)S(1)} %bitcast.816, pred[2,256,1024]{1,2,0:T(8,128)(4,1)S(1)} %compare_and_fusion, bf16[2,256,2,4,128]{1,4,3,2,0:T(8,128)(2,1)} %copy.696, ...), kind=kOutput, calls=%fused_computation.8 | convolution fusion | flops 1094709248 | bytes 36208640 | tf_op jit(solution)/shard_map/sikgd,sjkd->skgij/dot_general | solution.py:466
  502.6 11.1 %fusion.4 = bf16[2,2,4,256,1024]{3,4,2,1,0:T(8,128)(2,1)} fusion(f32[2,2,1024,256,4]{3,2,4,1,0:T(8,128)} %get-tuple-element.693, f32[2,2,1024,256,4]{3,2,4,1,0:T(8,128)S(1)} %bitcast.728, f32[2,2,4,256]{3,2,1,0:T(4,128)S(1)} %get-tuple-element.692, f32[2,2,4,256]{3,2,1,0:T(4,128)S(1)} %bitcast.817, pred[2,256,1024]{1,2,0:T(8,128)(4,1)S(1)} %compare_and_fusion), kind=kLoop, calls=%fused_computation.10 | loop fusion | flops 25165824 | bytes 42500096 | tf_op jit(solution)/shard_map/convert_element_type | solution.py:473
  513.7 7.7 fusion.117
  528.6 6.7 constant_dynamic-slice_fusion.3
  544.5 17.1 %fusion.17 = (f32[2,256,24]{1,2,0:T(8,128)S(1)}, f32[2,256,24]{1,2,0:T(8,128)}, f32[2,256,24]{1,2,0:T(8,128)}, f32[2,256,256]{2,1,0:T(8,128)}) fusion(f32[2,256,24]{1,2,0:T(8,128)} %copy.647, f32[2,256,24]{1,2,0:T(8,128)} %copy.645, f32[2,256,256]{2,1,0:T(8,128)} %fusion.162, pred[2,256,256]{2,1,0:T(8,128)(4,1)S(1)} %copy-done.129, ...), kind=kOutput, calls=%fused_computation.30 | convolution fusion | flops 1254977536 | bytes 7716864 | tf_op jit(solution)/shard_map/transpose(jvp(vmap(ijh,jhp->ihp)))/dot_general | solution.py:225
  564.1 5.0 reduce-window.34
  605.8 6.7 fusion.105
  612.5 6.8 collective-permute-done.38
  639.2 15.9 %collective-permute-done.65 = bf16[2,2,2,32,2048]{4,3,0,1,2:T(8,128)(2,1)S(1)} collective-permute-done((bf16[2,2,2,32,2048]{4,3,0,1,2:T(8,128)(2,1)S(1)}, bf16[2,2,2,32,2048]{4,3,0,1,2:T(8,128)(2,1)S(1)}, u32[]{:S(2)}, u32[]{:S(2)}) %collective-permute-start.65) | collective-permute-done | bytes 1048608 | tf_op jit(solution)/shard_map/ppermute | solution.py:42
  658.3 20.9 %collective-permute-done.70 = bf16[2,2,2,64,1024]{4,3,0,1,2:T(8,128)(2,1)S(1)} collective-permute-done((bf16[2,2,2,64,1024]{4,3,0,1,2:T(8,128)(2,1)S(1)}, bf16[2,2,2,64,1024]{4,3,0,1,2:T(8,128)(2,1)S(1)}, u32[]{:S(2)}, u32[]{:S(2)}) %collective-permute-start.70) | collective-permute-done | bytes 1048608 | tf_op jit(solution)/shard_map/ppermute | solution.py:42
  680.3 37.5 %collective-permute-done.66 = bf16[2,2,32,2048]{3,2,0,1:T(8,128)(2,1)S(1)} collective-permute-done((bf16[2,2,32,2048]{3,2,0,1:T(8,128)(2,1)S(1)}, bf16[2,2,32,2048]{3,2,0,1:T(8,128)(2,1)S(1)}, u32[]{:S(2)}, u32[]{:S(2)}) %collective-permute-start.66) | collective-permute-done | bytes 524320 | tf_op jit(solution)/shard_map/ppermute | solution.py:42
  723.0 13.2 %collective-permute-done.46 = bf16[2,2,32,2560]{3,2,0,1:T(8,128)(2,1)S(1)} collective-permute-done((bf16[2,2,32,2560]{3,2,0,1:T(8,128)(2,1)S(1)}, bf16[2,2,32,2560]{3,2,0,1:T(8,128)(2,1)S(1)}, u32[]{:S(2)}, u32[]{:S(2)}) %collective-permute-start.46) | collective-permute-done | bytes 655392 | tf_op jit(solution)/shard_map/ppermute | solution.py:42
  739.7 9.0 while.32
  758.6 8.1 fusion.54
  769.1 12.0 %multiply_reduce_fusion.3 = (f32[1792]{0:T(1024)S(1)}, f32[1792]{0:T(1024)}, f32[1792]{0:T(1024)S(1)}, f32[1792]{0:T(1024)S(1)}, bf16[1792]{0:T(1024)(128)(2,1)}, /*index=5*/f32[2,256,1792]{2,1,0:T(8,128)}) fusion(f32[2,256,1792]{2,1,0:T(8,128)} %bitcast.742, f32[2,3,1792]{2,1,0:T(4,128)} %collective-permute-done.11, pred[2,256]{1,0:T(4,128)(4,1)} %get-tuple-element.667, ...), kind=kLoop, calls=%fused_computation.100 | loop fusion | flops 24763648 | bytes 18427392 | tf_op jit(solution)/shard_map/transpose(jvp())/reduce_sum | solution.py:195
  784.5 5.0 reduce-window.36
  832.3 6.8 convolution_convert_fusion
  839.1 7.5 fusion.95
  874.8 20.8 %collective-permute-done.40 = bf16[2,2,2,32,2432]{4,3,0,1,2:T(8,128)(2,1)S(1)} collective-permute-done((bf16[2,2,2,32,2432]{4,3,0,1,2:T(8,128)(2,1)S(1)}, bf16[2,2,2,32,2432]{4,3,0,1,2:T(8,128)(2,1)S(1)}, u32[]{:S(2)}, u32[]{:S(2)}) %collective-permute-start.40) | collective-permute-done | bytes 1245216 | tf_op jit(solution)/shard_map/ppermute | solution.py:42
  902.1 8.8 collective-permute-done.41
  913.2 6.4 collective-permute-done.42
  922.3 5.2 collective-permute-done.43
  (931 shorter events, 478.8 us)
Async XLA Ops:
  7.2 358.5 %all-gather.5.cloned.1.call-start = ((), (), s32[]{:S(2)}) async-start(), calls=%async_computation | async-start | bytes 3932160 | tf_op jit(solution)/shard_map/all_gather | solution.py:98
  8.0 22.4 %collective-permute-start.10 = (f32[2,3]{1,0:T(2,128)S(1)}, f32[2,3]{1,0:T(2,128)S(1)}, u32[]{:S(2)}, u32[]{:S(2)}) collective-permute-start(f32[2,3]{1,0:T(2,128)S(1)} %slice.331), channel_id=1, source_target_pairs={{0,1},{1,2},{2,3},{4,5},{5,6},{6,7},{8,9},{9,10},{10,11},{12,13},{... | collective-permute-start | bytes 80 | tf_op jit(solution)/shard_map/ppermute | solution.py:24
  10.3 90.3 %collective-permute-start.19 = (bf16[2,256]{1,0:T(2,128)(2,1)S(1)}, bf16[2,256]{1,0:T(2,128)(2,1)S(1)}, u32[]{:S(2)}, u32[]{:S(2)}) collective-permute-start(bf16[2,256]{1,0:T(2,128)(2,1)S(1)} %get-tuple-element.679), channel_id=1, source_target_pairs={{0,2},{1,3},{2,0},{3,1},{4,6},{5,7},{6,4},{7,5},{8,10},{9,11},{10,... | collective-permute-start | bytes 3080 | tf_op jit(solution)/shard_map/ppermute | solution.py:42
  49.5 17.7 %collective-permute-start.2 = (bf16[2,2,32,2560]{3,2,1,0:T(8,128)(2,1)S(1)}, bf16[2,2,32,2560]{3,2,1,0:T(8,128)(2,1)S(1)}, u32[]{:S(2)}, u32[]{:S(2)}) collective-permute-start(bf16[2,2,32,2560]{3,2,1,0:T(8,128)(2,1)S(1)} %pad_maximum_fusion.27), channel_id=1, source_target_pairs={{0,4},{4,0},{8,12},{12,8},{16,20},{20,16},{24,28},{28,24},{1,5},{5... | collective-permute-start | bytes 1966088 | tf_op jit(solution)/shard_map/ppermute | solution.py:42
  59.2 31.8 %collective-permute-start.8 = (bf16[2,2,2,32,2432]{4,3,2,1,0:T(8,128)(2,1)S(1)}, bf16[2,2,2,32,2432]{4,3,2,1,0:T(8,128)(2,1)S(1)}, u32[]{:S(2)}, u32[]{:S(2)}) collective-permute-start(bf16[2,2,2,32,2432]{4,3,2,1,0:T(8,128)(2,1)S(1)} %pad_maximum_fusion.20), channel_id=1, source_target_pairs={{0,4},{4,0},{8,12},{12,8},{16,20},{20,16},{24,28},{28,24},{1,5},{5... | collective-permute-start | bytes 3735560 | tf_op jit(solution)/shard_map/ppermute | solution.py:42
  67.5 29.4 %collective-permute-start.3 = (bf16[2,2,2,32,2560]{4,3,2,1,0:T(8,128)(2,1)S(1)}, bf16[2,2,2,32,2560]{4,3,2,1,0:T(8,128)(2,1)S(1)}, u32[]{:S(2)}, u32[]{:S(2)}) collective-permute-start(bf16[2,2,2,32,2560]{4,3,2,1,0:T(8,128)(2,1)S(1)} %pad_maximum_fusion.18), channel_id=1, source_target_pairs={{0,2},{1,3},{2,0},{3,1},{4,6},{5,7},{6,4},{7,5},{8,10},{9,11},{10,... | collective-permute-start | bytes 3932168 | tf_op jit(solution)/shard_map/ppermute | solution.py:42
  143.8 94.7 %collective-permute-start.21 = (bf16[32,2048]{1,0:T(8,128)(2,1)}, bf16[32,2048]{1,0:T(8,128)(2,1)}, u32[]{:S(2)}, u32[]{:S(2)}) collective-permute-start(bf16[32,2048]{1,0:T(8,128)(2,1)} %param.46), channel_id=1, source_target_pairs={{0,16},{4,20},{8,24},{12,28},{16,0},{20,4},{24,8},{28,12},{1,17},{... | collective-permute-start | bytes 393224 | tf_op jit(solution)/shard_map/ppermute | solution.py:42
  144.7 94.8 %collective-permute-start.26 = (bf16[32,2048]{1,0:T(8,128)(2,1)}, bf16[32,2048]{1,0:T(8,128)(2,1)}, u32[]{:S(2)}, u32[]{:S(2)}) collective-permute-start(bf16[32,2048]{1,0:T(8,128)(2,1)} %param.47), channel_id=1, source_target_pairs={{0,16},{4,20},{8,24},{12,28},{16,0},{20,4},{24,8},{28,12},{1,17},{... | collective-permute-start | bytes 393224 | tf_op jit(solution)/shard_map/ppermute | solution.py:42
  146.7 96.0 %collective-permute-start.31 = (bf16[64,1024]{1,0:T(8,128)(2,1)}, bf16[64,1024]{1,0:T(8,128)(2,1)}, u32[]{:S(2)}, u32[]{:S(2)}) collective-permute-start(bf16[64,1024]{1,0:T(8,128)(2,1)} %param.48), channel_id=1, source_target_pairs={{0,16},{4,20},{8,24},{12,28},{16,0},{20,4},{24,8},{28,12},{1,17},{... | collective-permute-start | bytes 393224 | tf_op jit(solution)/shard_map/ppermute | solution.py:42
  148.9 94.9 %collective-permute-start.12 = (bf16[80,1024]{1,0:T(8,128)(2,1)}, bf16[80,1024]{1,0:T(8,128)(2,1)}, u32[]{:S(2)}, u32[]{:S(2)}) collective-permute-start(bf16[80,1024]{1,0:T(8,128)(2,1)} %constant_dynamic-update-slice_fusion.2), channel_id=1, source_target_pairs={{0,16},{4,20},{8,24},{12,28},{16,0},{20,4},{24,8},{28,12},{1,17},{... | collective-permute-start | bytes 491528 | tf_op jit(solution)/shard_map/ppermute | solution.py:42
  162.6 39.3 %collective-permute-start.11 = (f32[2,3,1792]{2,1,0:T(4,128)}, f32[2,3,1792]{2,1,0:T(4,128)}, u32[]{:S(2)}, u32[]{:S(2)}) collective-permute-start(f32[2,3,1792]{2,1,0:T(4,128)} %slice.336), channel_id=1, source_target_pairs={{0,1},{1,2},{2,3},{4,5},{5,6},{6,7},{8,9},{9,10},{10,11},{12,13},{... | collective-permute-start | bytes 129032 | tf_op jit(solution)/shard_map/ppermute | solution.py:24
  201.9 64.9 %collective-permute-start.17 = (bf16[2,256,4,128]{3,1,2,0:T(8,128)(2,1)}, bf16[2,256,4,128]{3,1,2,0:T(8,128)(2,1)}, u32[]{:S(2)}, u32[]{:S(2)}) collective-permute-start(bf16[2,256,4,128]{3,1,2,0:T(8,128)(2,1)} %pad_maximum_fusion.30), channel_id=1, source_target_pairs={{0,2},{1,3},{2,0},{3,1},{4,6},{5,7},{6,4},{7,5},{8,10},{9,11},{10,... | collective-permute-start | bytes 1572872 | tf_op jit(solution)/shard_map/ppermute | solution.py:42
  226.5 513.2 %all-gather.7.cloned.1.call-start = ((), (), s32[]{:S(2)}) async-start(), calls=%async_computation.1 | async-start | bytes 3932160 | tf_op jit(solution)/shard_map/all_gather | solution.py:121
  244.8 21.2 %collective-permute-start.13 = (bf16[2,80,1024]{2,1,0:T(8,128)(2,1)S(1)}, bf16[2,80,1024]{2,1,0:T(8,128)(2,1)S(1)}, u32[]{:S(2)}, u32[]{:S(2)}) collective-permute-start(bf16[2,80,1024]{2,1,0:T(8,128)(2,1)S(1)} %pad_maximum_fusion.35), channel_id=1, source_target_pairs={{0,8},{4,12},{8,0},{12,4},{16,24},{20,28},{24,16},{28,20},{1,9},{5... | collective-permute-start | bytes 983048 | tf_op jit(solution)/shard_map/ppermute | solution.py:42
  248.8 19.6 %collective-permute-start.23 = (bf16[2,2,32,2048]{3,2,0,1:T(8,128)(2,1)S(1)}, bf16[2,2,32,2048]{3,2,0,1:T(8,128)(2,1)S(1)}, u32[]{:S(2)}, u32[]{:S(2)}) collective-permute-start(bf16[2,2,32,2048]{3,2,0,1:T(8,128)(2,1)S(1)} %pad_maximum_fusion.31), channel_id=1, source_target_pairs={{0,4},{4,0},{8,12},{12,8},{16,20},{20,16},{24,28},{28,24},{1,5},{5... | collective-permute-start | bytes 1572872 | tf_op jit(solution)/shard_map/ppermute | solution.py:42
  268.3 19.1 %collective-permute-start.18 = (bf16[2,2,256,4,128]{4,2,3,1,0:T(8,128)(2,1)S(1)}, bf16[2,2,256,4,128]{4,2,3,1,0:T(8,128)(2,1)S(1)}, u32[]{:S(2)}, u32[]{:S(2)}) collective-permute-start(bf16[2,2,256,4,128]{4,2,3,1,0:T(8,128)(2,1)S(1)} %pad_maximum_fusion.21), channel_id=1, source_target_pairs={{0,1},{1,0},{2,3},{3,2},{4,5},{5,4},{6,7},{7,6},{8,9},{9,8},{10,11... | collective-permute-start | bytes 3145736 | tf_op jit(solution)/shard_map/ppermute | solution.py:42
  269.7 37.2 %collective-permute-start.24 = (bf16[2,2,2,32,2048]{4,3,0,1,2:T(8,128)(2,1)}, bf16[2,2,2,32,2048]{4,3,0,1,2:T(8,128)(2,1)}, u32[]{:S(2)}, u32[]{:S(2)}) collective-permute-start(bf16[2,2,2,32,2048]{4,3,0,1,2:T(8,128)(2,1)} %pad_maximum_fusion.23), channel_id=1, source_target_pairs={{0,2},{1,3},{2,0},{3,1},{4,6},{5,7},{6,4},{7,5},{8,10},{9,11},{10,... | collective-permute-start | bytes 3145736 | tf_op jit(solution)/shard_map/ppermute | solution.py:42
  272.4 38.2 %collective-permute-start.29 = (bf16[2,2,2,32,2048]{4,3,2,1,0:T(8,128)(2,1)}, bf16[2,2,2,32,2048]{4,3,2,1,0:T(8,128)(2,1)}, u32[]{:S(2)}, u32[]{:S(2)}) collective-permute-start(bf16[2,2,2,32,2048]{4,3,2,1,0:T(8,128)(2,1)} %pad_maximum_fusion.24), channel_id=1, source_target_pairs={{0,4},{4,0},{8,12},{12,8},{16,20},{20,16},{24,28},{28,24},{1,5},{5... | collective-permute-start | bytes 3145736 | tf_op jit(solution)/shard_map/ppermute | solution.py:42
  275.0 52.0 %collective-permute-start.34 = (bf16[2,2,2,64,1024]{4,3,2,1,0:T(8,128)(2,1)}, bf16[2,2,2,64,1024]{4,3,2,1,0:T(8,128)(2,1)}, u32[]{:S(2)}, u32[]{:S(2)}) collective-permute-start(bf16[2,2,2,64,1024]{4,3,2,1,0:T(8,128)(2,1)} %pad_maximum_fusion.25), channel_id=1, source_target_pairs={{0,2},{1,3},{2,0},{3,1},{4,6},{5,7},{6,4},{7,5},{8,10},{9,11},{10,... | collective-permute-start | bytes 3145736 | tf_op jit(solution)/shard_map/ppermute | solution.py:42
  286.0 56.3 %collective-permute-start.15 = (bf16[2,2,2,80,1024]{4,3,2,1,0:T(8,128)(2,1)}, bf16[2,2,2,80,1024]{4,3,2,1,0:T(8,128)(2,1)}, u32[]{:S(2)}, u32[]{:S(2)}) collective-permute-start(bf16[2,2,2,80,1024]{4,3,2,1,0:T(8,128)(2,1)} %pad_maximum_fusion.19), channel_id=1, source_target_pairs={{0,4},{4,0},{8,12},{12,8},{16,20},{20,16},{24,28},{28,24},{1,5},{5... | collective-permute-start | bytes 3932168 | tf_op jit(solution)/shard_map/ppermute | solution.py:42
  310.6 43.9 %collective-permute-start.25 = (bf16[2,2,2,2,32,2048]{5,4,3,2,1,0:T(8,128)(2,1)}, bf16[2,2,2,2,32,2048]{5,4,3,2,1,0:T(8,128)(2,1)}, u32[]{:S(2)}, u32[]{:S(2)}) collective-permute-start(bf16[2,2,2,2,32,2048]{5,4,3,2,1,0:T(8,128)(2,1)} %copy.762), channel_id=1, source_target_pairs={{0,1},{1,0},{2,3},{3,2},{4,5},{5,4},{6,7},{7,6},{8,9},{9,8},{10,11... | collective-permute-start | bytes 6291464 | tf_op jit(solution)/shard_map/ppermute | solution.py:42
  313.7 33.6 %collective-permute-start.30 = (bf16[2,2,2,2,32,2048]{5,4,3,2,1,0:T(8,128)(2,1)}, bf16[2,2,2,2,32,2048]{5,4,3,2,1,0:T(8,128)(2,1)}, u32[]{:S(2)}, u32[]{:S(2)}) collective-permute-start(bf16[2,2,2,2,32,2048]{5,4,3,2,1,0:T(8,128)(2,1)} %pad_maximum_fusion.13), channel_id=1, source_target_pairs={{0,1},{1,0},{2,3},{3,2},{4,5},{5,4},{6,7},{7,6},{8,9},{9,8},{10,11... | collective-permute-start | bytes 6291464 | tf_op jit(solution)/shard_map/ppermute | solution.py:42
  331.0 21.2 %collective-permute-start.35 = (bf16[2,2,2,2,64,1024]{5,4,3,2,1,0:T(8,128)(2,1)}, bf16[2,2,2,2,64,1024]{5,4,3,2,1,0:T(8,128)(2,1)}, u32[]{:S(2)}, u32[]{:S(2)}) collective-permute-start(bf16[2,2,2,2,64,1024]{5,4,3,2,1,0:T(8,128)(2,1)} %pad_maximum_fusion.14), channel_id=1, source_target_pairs={{0,1},{1,0},{2,3},{3,2},{4,5},{5,4},{6,7},{7,6},{8,9},{9,8},{10,11... | collective-permute-start | bytes 6291464 | tf_op jit(solution)/shard_map/ppermute | solution.py:42
  346.8 60.6 %collective-permute-start.16 = (bf16[2,2,2,2,80,1024]{5,4,3,2,1,0:T(8,128)(2,1)}, bf16[2,2,2,2,80,1024]{5,4,3,2,1,0:T(8,128)(2,1)}, u32[]{:S(2)}, u32[]{:S(2)}) collective-permute-start(bf16[2,2,2,2,80,1024]{5,4,3,2,1,0:T(8,128)(2,1)} %pad_maximum_fusion.8), channel_id=1, source_target_pairs={{0,1},{1,0},{2,3},{3,2},{4,5},{5,4},{6,7},{7,6},{8,9},{9,8},{10,11... | collective-permute-start | bytes 7864328 | tf_op jit(solution)/shard_map/ppermute | solution.py:42
  538.4 85.5 %collective-permute-start.59 = (bf16[2,2,2,2,32,2048]{5,4,0,1,2,3:T(8,128)(2,1)}, bf16[2,2,2,2,32,2048]{5,4,0,1,2,3:T(8,128)(2,1)}, u32[]{:S(2)}, u32[]{:S(2)}) collective-permute-start(bf16[2,2,2,2,32,2048]{5,4,0,1,2,3:T(8,128)(2,1)} %bitcast.713), channel_id=1, source_target_pairs={{0,1},{1,0},{2,3},{3,2},{4,5},{5,4},{6,7},{7,6},{8,9},{9,8},{10,11... | collective-permute-start | bytes 6291464 | tf_op jit(solution)/shard_map/ppermute | solution.py:42
  538.7 82.6 %collective-permute-start.64 = (bf16[2,2,2,2,32,2048]{5,4,0,1,3,2:T(8,128)(2,1)}, bf16[2,2,2,2,32,2048]{5,4,0,1,3,2:T(8,128)(2,1)}, u32[]{:S(2)}, u32[]{:S(2)}) collective-permute-start(bf16[2,2,2,2,32,2048]{5,4,0,1,3,2:T(8,128)(2,1)} %bitcast.712), channel_id=1, source_target_pairs={{0,1},{1,0},{2,3},{3,2},{4,5},{5,4},{6,7},{7,6},{8,9},{9,8},{10,11... | collective-permute-start | bytes 6291464 | tf_op jit(solution)/shard_map/ppermute | solution.py:42
  543.3 89.6 %collective-permute-start.54 = (bf16[2,2,2,2,80,1024]{5,4,0,1,3,2:T(8,128)(2,1)}, bf16[2,2,2,2,80,1024]{5,4,0,1,3,2:T(8,128)(2,1)}, u32[]{:S(2)}, u32[]{:S(2)}) collective-permute-start(bf16[2,2,2,2,80,1024]{5,4,0,1,3,2:T(8,128)(2,1)} %bitcast.708), channel_id=1, source_target_pairs={{0,1},{1,0},{2,3},{3,2},{4,5},{5,4},{6,7},{7,6},{8,9},{9,8},{10,11... | collective-permute-start | bytes 7864328 | tf_op jit(solution)/shard_map/ppermute | solution.py:42
  576.6 49.8 %collective-permute-start.69 = (bf16[2,2,2,2,64,1024]{5,4,0,1,2,3:T(8,128)(2,1)}, bf16[2,2,2,2,64,1024]{5,4,0,1,2,3:T(8,128)(2,1)}, u32[]{:S(2)}, u32[]{:S(2)}) collective-permute-start(bf16[2,2,2,2,64,1024]{5,4,0,1,2,3:T(8,128)(2,1)} %bitcast.711), channel_id=1, source_target_pairs={{0,1},{1,0},{2,3},{3,2},{4,5},{5,4},{6,7},{7,6},{8,9},{9,8},{10,11... | collective-permute-start | bytes 6291464 | tf_op jit(solution)/shard_map/ppermute | solution.py:42
  579.7 23.1 %collective-permute-start.37 = (bf16[2,2,256,4,128]{4,2,3,1,0:T(8,128)(2,1)}, bf16[2,2,256,4,128]{4,2,3,1,0:T(8,128)(2,1)}, u32[]{:S(2)}, u32[]{:S(2)}) collective-permute-start(bf16[2,2,256,4,128]{4,2,3,1,0:T(8,128)(2,1)} %dynamic-slice_bitcast_fusion.6), channel_id=1, source_target_pairs={{0,1},{1,0},{2,3},{3,2},{4,5},{5,4},{6,7},{7,6},{8,9},{9,8},{10,11... | collective-permute-start | bytes 3145736 | tf_op jit(solution)/shard_map/ppermute | solution.py:42
  629.1 26.0 %collective-permute-start.65 = (bf16[2,2,2,32,2048]{4,3,0,1,2:T(8,128)(2,1)S(1)}, bf16[2,2,2,32,2048]{4,3,0,1,2:T(8,128)(2,1)S(1)}, u32[]{:S(2)}, u32[]{:S(2)}) collective-permute-start(bf16[2,2,2,32,2048]{4,3,0,1,2:T(8,128)(2,1)S(1)} %dynamic-slice_bitcast_fusion.4), channel_id=1, source_target_pairs={{0,4},{4,0},{8,12},{12,8},{16,20},{20,16},{24,28},{28,24},{1,5},{5... | collective-permute-start | bytes 3145736 | tf_op jit(solution)/shard_map/ppermute | solution.py:42
  630.7 26.1 %collective-permute-start.60 = (bf16[2,2,2,32,2048]{4,3,0,1,2:T(8,128)(2,1)S(1)}, bf16[2,2,2,32,2048]{4,3,0,1,2:T(8,128)(2,1)S(1)}, u32[]{:S(2)}, u32[]{:S(2)}) collective-permute-start(bf16[2,2,2,32,2048]{4,3,0,1,2:T(8,128)(2,1)S(1)} %dynamic-slice_bitcast_fusion.5), channel_id=1, source_target_pairs={{0,2},{1,3},{2,0},{3,1},{4,6},{5,7},{6,4},{7,5},{8,10},{9,11},{10,... | collective-permute-start | bytes 3145736 | tf_op jit(solution)/shard_map/ppermute | solution.py:42
  631.3 47.9 %collective-permute-start.70 = (bf16[2,2,2,64,1024]{4,3,0,1,2:T(8,128)(2,1)S(1)}, bf16[2,2,2,64,1024]{4,3,0,1,2:T(8,128)(2,1)S(1)}, u32[]{:S(2)}, u32[]{:S(2)}) collective-permute-start(bf16[2,2,2,64,1024]{4,3,0,1,2:T(8,128)(2,1)S(1)} %dynamic-slice_bitcast_fusion.3), channel_id=1, source_target_pairs={{0,2},{1,3},{2,0},{3,1},{4,6},{5,7},{6,4},{7,5},{8,10},{9,11},{10,... | collective-permute-start | bytes 3145736 | tf_op jit(solution)/shard_map/ppermute | solution.py:42
  636.0 85.7 %collective-permute-start.55 = (bf16[2,2,2,80,1024]{4,3,0,1,2:T(8,128)(2,1)S(1)}, bf16[2,2,2,80,1024]{4,3,0,1,2:T(8,128)(2,1)S(1)}, u32[]{:S(2)}, u32[]{:S(2)}) collective-permute-start(bf16[2,2,2,80,1024]{4,3,0,1,2:T(8,128)(2,1)S(1)} %dynamic-slice_bitcast_fusion), channel_id=1, source_target_pairs={{0,4},{4,0},{8,12},{12,8},{16,20},{20,16},{24,28},{28,24},{1,5},{5... | collective-permute-start | bytes 3932168 | tf_op jit(solution)/shard_map/ppermute | solution.py:42
  638.6 81.1 %collective-permute-start.45 = (bf16[2,2,2,32,2560]{4,3,0,1,2:T(8,128)(2,1)S(1)}, bf16[2,2,2,32,2560]{4,3,0,1,2:T(8,128)(2,1)S(1)}, u32[]{:S(2)}, u32[]{:S(2)}) collective-permute-start(bf16[2,2,2,32,2560]{4,3,0,1,2:T(8,128)(2,1)S(1)} %dynamic-slice_bitcast_fusion.1), channel_id=1, source_target_pairs={{0,2},{1,3},{2,0},{3,1},{4,6},{5,7},{6,4},{7,5},{8,10},{9,11},{10,... | collective-permute-start | bytes 3932168 | tf_op jit(solution)/shard_map/ppermute | solution.py:42
  655.7 62.1 %collective-permute-start.66 = (bf16[2,2,32,2048]{3,2,0,1:T(8,128)(2,1)S(1)}, bf16[2,2,32,2048]{3,2,0,1:T(8,128)(2,1)S(1)}, u32[]{:S(2)}, u32[]{:S(2)}) collective-permute-start(bf16[2,2,32,2048]{3,2,0,1:T(8,128)(2,1)S(1)} %dynamic-slice_bitcast_fusion.11), channel_id=1, source_target_pairs={{0,2},{1,3},{2,0},{3,1},{4,6},{5,7},{6,4},{7,5},{8,10},{9,11},{10,... | collective-permute-start | bytes 1572872 | tf_op jit(solution)/shard_map/ppermute | solution.py:42
  657.2 61.6 %collective-permute-start.61 = (bf16[2,2,32,2048]{3,2,0,1:T(8,128)(2,1)S(1)}, bf16[2,2,32,2048]{3,2,0,1:T(8,128)(2,1)S(1)}, u32[]{:S(2)}, u32[]{:S(2)}) collective-permute-start(bf16[2,2,32,2048]{3,2,0,1:T(8,128)(2,1)S(1)} %dynamic-slice_bitcast_fusion.12), channel_id=1, source_target_pairs={{0,4},{4,0},{8,12},{12,8},{16,20},{20,16},{24,28},{28,24},{1,5},{5... | collective-permute-start | bytes 1572872 | tf_op jit(solution)/shard_map/ppermute | solution.py:42
  679.7 41.1 %collective-permute-start.71 = (bf16[2,2,64,1024]{3,2,0,1:T(8,128)(2,1)S(1)}, bf16[2,2,64,1024]{3,2,0,1:T(8,128)(2,1)S(1)}, u32[]{:S(2)}, u32[]{:S(2)}) collective-permute-start(bf16[2,2,64,1024]{3,2,0,1:T(8,128)(2,1)S(1)} %dynamic-slice_bitcast_fusion.10), channel_id=1, source_target_pairs={{0,4},{4,0},{8,12},{12,8},{16,20},{20,16},{24,28},{28,24},{1,5},{5... | collective-permute-start | bytes 1572872 | tf_op jit(solution)/shard_map/ppermute | solution.py:42
  738.0 123.6 %collective-permute-start.47 = (bf16[2,32,2560]{2,1,0:T(8,128)(2,1)}, bf16[2,32,2560]{2,1,0:T(8,128)(2,1)}, u32[]{:S(2)}, u32[]{:S(2)}) collective-permute-start(bf16[2,32,2560]{2,1,0:T(8,128)(2,1)} %dynamic-slice_bitcast_fusion.15), channel_id=1, source_target_pairs={{0,8},{4,12},{8,0},{12,4},{16,24},{20,28},{24,16},{28,20},{1,9},{5... | collective-permute-start | bytes 983048 | tf_op jit(solution)/shard_map/ppermute | solution.py:42
  799.9 29.1 %collective-permute-start.36 = (bf16[2,3,1792]{2,1,0:T(4,128)(2,1)}, bf16[2,3,1792]{2,1,0:T(4,128)(2,1)}, u32[]{:S(2)}, u32[]{:S(2)}) collective-permute-start(bf16[2,3,1792]{2,1,0:T(4,128)(2,1)} %slice.511), channel_id=1, source_target_pairs={{1,0},{2,1},{3,2},{5,4},{6,5},{7,6},{9,8},{10,9},{11,10},{13,12},{... | collective-permute-start | bytes 64520 | tf_op jit(solution)/shard_map/ppermute | solution.py:24
  801.9 61.6 %collective-permute-start.67 = (bf16[2,32,2048]{2,1,0:T(8,128)(2,1)}, bf16[2,32,2048]{2,1,0:T(8,128)(2,1)}, u32[]{:S(2)}, u32[]{:S(2)}) collective-permute-start(bf16[2,32,2048]{2,1,0:T(8,128)(2,1)} %dynamic-slice_bitcast_fusion.18), channel_id=1, source_target_pairs={{0,8},{4,12},{8,0},{12,4},{16,24},{20,28},{24,16},{28,20},{1,9},{5... | collective-permute-start | bytes 786440 | tf_op jit(solution)/shard_map/ppermute | solution.py:42
  804.1 64.3 %collective-permute-start.62 = (bf16[2,32,2048]{2,1,0:T(8,128)(2,1)}, bf16[2,32,2048]{2,1,0:T(8,128)(2,1)}, u32[]{:S(2)}, u32[]{:S(2)}) collective-permute-start(bf16[2,32,2048]{2,1,0:T(8,128)(2,1)} %dynamic-slice_bitcast_fusion.19), channel_id=1, source_target_pairs={{0,8},{4,12},{8,0},{12,4},{16,24},{20,28},{24,16},{28,20},{1,9},{5... | collective-permute-start | bytes 786440 | tf_op jit(solution)/shard_map/ppermute | solution.py:42
  826.4 44.0 %collective-permute-start.72 = (bf16[2,64,1024]{2,1,0:T(8,128)(2,1)}, bf16[2,64,1024]{2,1,0:T(8,128)(2,1)}, u32[]{:S(2)}, u32[]{:S(2)}) collective-permute-start(bf16[2,64,1024]{2,1,0:T(8,128)(2,1)} %dynamic-slice_bitcast_fusion.17), channel_id=1, source_target_pairs={{0,8},{4,12},{8,0},{12,4},{16,24},{20,28},{24,16},{28,20},{1,9},{5... | collective-permute-start | bytes 786440 | tf_op jit(solution)/shard_map/ppermute | solution.py:42
  863.5 34.4 %collective-permute-start.48 = (bf16[32,2560]{1,0:T(8,128)(2,1)S(1)}, bf16[32,2560]{1,0:T(8,128)(2,1)S(1)}, u32[]{:S(2)}, u32[]{:S(2)}) collective-permute-start(bf16[32,2560]{1,0:T(8,128)(2,1)S(1)} %dynamic-slice_bitcast_fusion.21), channel_id=1, source_target_pairs={{0,16},{4,20},{8,24},{12,28},{16,0},{20,4},{24,8},{28,12},{1,17},{... | collective-permute-start | bytes 491528 | tf_op jit(solution)/shard_map/ppermute | solution.py:42
  866.5 34.8 %collective-permute-start.68 = (bf16[32,2048]{1,0:T(8,128)(2,1)S(1)}, bf16[32,2048]{1,0:T(8,128)(2,1)S(1)}, u32[]{:S(2)}, u32[]{:S(2)}) collective-permute-start(bf16[32,2048]{1,0:T(8,128)(2,1)S(1)} %dynamic-slice_bitcast_fusion.24), channel_id=1, source_target_pairs={{0,16},{4,20},{8,24},{12,28},{16,0},{20,4},{24,8},{28,12},{1,17},{... | collective-permute-start | bytes 393224 | tf_op jit(solution)/shard_map/ppermute | solution.py:42
  868.4 27.3 %collective-permute-start.40 = (bf16[2,2,2,32,2432]{4,3,0,1,2:T(8,128)(2,1)S(1)}, bf16[2,2,2,32,2432]{4,3,0,1,2:T(8,128)(2,1)S(1)}, u32[]{:S(2)}, u32[]{:S(2)}) collective-permute-start(bf16[2,2,2,32,2432]{4,3,0,1,2:T(8,128)(2,1)S(1)} %dynamic-slice_bitcast_fusion.2), channel_id=1, source_target_pairs={{0,4},{4,0},{8,12},{12,8},{16,20},{20,16},{24,28},{28,24},{1,5},{5... | collective-permute-start | bytes 3735560 | tf_op jit(solution)/shard_map/ppermute | solution.py:42
  870.4 41.4 %collective-permute-start.63 = (bf16[32,2048]{1,0:T(8,128)(2,1)S(1)}, bf16[32,2048]{1,0:T(8,128)(2,1)S(1)}, u32[]{:S(2)}, u32[]{:S(2)}) collective-permute-start(bf16[32,2048]{1,0:T(8,128)(2,1)S(1)} %dynamic-slice_bitcast_fusion.25), channel_id=1, source_target_pairs={{0,16},{4,20},{8,24},{12,28},{16,0},{20,4},{24,8},{28,12},{1,17},{... | collective-permute-start | bytes 393224 | tf_op jit(solution)/shard_map/ppermute | solution.py:42
  874.5 38.0 %collective-permute-start.73 = (bf16[64,1024]{1,0:T(8,128)(2,1)S(1)}, bf16[64,1024]{1,0:T(8,128)(2,1)S(1)}, u32[]{:S(2)}, u32[]{:S(2)}) collective-permute-start(bf16[64,1024]{1,0:T(8,128)(2,1)S(1)} %dynamic-slice_bitcast_fusion.23), channel_id=1, source_target_pairs={{0,16},{4,20},{8,24},{12,28},{16,0},{20,4},{24,8},{28,12},{1,17},{... | collective-permute-start | bytes 393224 | tf_op jit(solution)/shard_map/ppermute | solution.py:42
  895.6 25.3 %collective-permute-start.58 = (bf16[80,1024]{1,0:T(8,128)(2,1)S(1)}, bf16[80,1024]{1,0:T(8,128)(2,1)S(1)}, u32[]{:S(2)}, u32[]{:S(2)}) collective-permute-start(bf16[80,1024]{1,0:T(8,128)(2,1)S(1)} %dynamic-slice_bitcast_fusion.20), channel_id=1, source_target_pairs={{0,16},{4,20},{8,24},{12,28},{16,0},{20,4},{24,8},{28,12},{1,17},{... | collective-permute-start | bytes 491528 | tf_op jit(solution)/shard_map/ppermute | solution.py:42
  (229 other events, 2518.7 us)
Sparse Core Ops, SparseCore 0:
  226.6 26.9 all-gather.4
  569.2 26.8 all-gather.6
